TPU v7x, 768 devices: a whole 4x8x12 slice. The times are simulated.
768 devices in a mesh: blk: 16 (over x, z_lo), table: 48 (over y, z_hi, core).
Axes of the slice: x: 4, y: 8, z: 12 (z_hi: 3, z_lo: 4; z = z_hi * 4 + z_lo), core: 2. Of those that a mesh axis runs over, the one named last changes fastest.
Arguments:
- id_table: bfloat16 [393216, 256], P('table'), may hold values from -6 to 6
- w_first: bfloat16 [256, 4096], replicated, may hold values from -0.375 to 0.375
- w_second: bfloat16 [4096, 256], replicated, may hold values from -0.09375 to 0.09375
- owner_ids: int32 [196608, 8], P(('blk', 'table')), may hold values from 0 to 47, all different within a row; in each aligned block of 256 rows (0 to 255, 256 to 511, ...) at most 64 rows name the same one
- row_ids: int32 [196608, 8], P(('blk', 'table')), may hold values from 0 to 8191
Outputs:
- loss: float32 [196608], P(('blk', 'table'))
- item_grad: float32 [196608, 256], P(('blk', 'table'))
- query_grad: float32 [196608, 256], P(('blk', 'table'))
Inputs may be any that keep to these rules, and one draw needn't show every extreme that they name: `owner_ids`: the 8 ids of one pair name 8 different shards; among the ids of one device's 256 pairs no shard is named more than 64 times, a bound that some block reaches.
All inputs are finite; a program needn't handle non-finite values.
Results may differ from a plain program's by a relative error of at most 0.0056.
Values may be sent and summed in bfloat16 or wider, within the bound.
A program may use at most 64 MiB of HBM per device.

v0:
```python
import jax
import jax.numpy as jnp
from jax import lax
from jax.sharding import PartitionSpec as P

EPS = 1e-06
INV_TEMP = 20.0


def shifted(shard, axis, by):
    count = lax.axis_size(axis)
    return lax.ppermute(shard, axis, [(i, (i + by) % count) for i in range(count)])


def silu_slope(pre):
    sigma = jax.nn.sigmoid(pre)
    return sigma * (1.0 + pre * (1.0 - sigma))


def unit_rows(vectors):
    scale = lax.rsqrt(jnp.sum(vectors * vectors, axis=-1, keepdims=True) + EPS)
    return (vectors * scale, scale)


def unit_backward(grad, unit, scale):
    return scale * (grad - unit * jnp.sum(unit * grad, axis=-1, keepdims=True))


def row_dot(left, right):
    return lax.dot_general(
        left, right, (((1,), (1,)), ((), ())), preferred_element_type=jnp.float32
    )


def col_dot(left, right):
    return lax.dot_general(
        left, right, (((0,), (0,)), ((), ())), preferred_element_type=jnp.float32
    )


def local(id_table, w_first, w_second, owner_ids, row_ids):
    pair_count, bags = owner_ids.shape
    half = bags // 2
    shards = lax.axis_size("table")
    width = id_table.shape[1]
    capacity = min(pair_count, 3 * pair_count * bags // (2 * shards))
    owners = owner_ids.reshape(-1)
    wanted_rows = row_ids.reshape(-1)
    onehot = (owners[:, None] == jnp.arange(shards, dtype=jnp.int32)[None, :]).astype(jnp.int32)
    earlier = jnp.cumsum(onehot, axis=0) - onehot
    slots = jnp.sum(earlier * onehot, axis=1)
    position = owners * capacity + slots
    requests = jnp.zeros((shards * capacity,), jnp.int32).at[position].set(wanted_rows)
    requests = requests.reshape(shards, capacity)
    found = jnp.take(
        id_table, lax.all_to_all(requests, "table", split_axis=0, concat_axis=0, tiled=True), axis=0
    )
    fetched = lax.all_to_all(found, "table", split_axis=0, concat_axis=0, tiled=True)
    embedded = jnp.take(fetched.reshape(shards * capacity, width), position, axis=0)
    embedded = embedded.reshape(pair_count, bags, width).astype(jnp.float32)
    query_in = jnp.sum(embedded[:, :half], axis=1).astype(jnp.bfloat16)
    item_in = jnp.sum(embedded[:, half:], axis=1)
    hidden_pre = jnp.dot(query_in, w_first, preferred_element_type=jnp.float32)
    hidden = jax.nn.silu(hidden_pre).astype(jnp.bfloat16)
    query_out = jnp.dot(hidden, w_second, preferred_element_type=jnp.float32)
    query_unit, query_scale = unit_rows(query_out)
    item_unit, item_scale = unit_rows(item_in)
    query_bf = query_unit.astype(jnp.bfloat16)
    item_bf = item_unit.astype(jnp.bfloat16)
    blocks = lax.axis_size("blk")

    def score_hop(hop_index, carry):
        visitor, exp_total = carry
        scores = INV_TEMP * row_dot(query_bf, visitor)
        exp_total = exp_total + jnp.sum(jnp.exp(scores), axis=1)
        visitor = shifted(visitor, "blk", 1)
        return (visitor, exp_total)

    returned, exp_total = lax.fori_loop(
        0, blocks, score_hop, (item_bf, jnp.zeros((pair_count,), jnp.float32))
    )
    log_total = jnp.log(exp_total)

    def grad_hop(hop_index, carry):
        visitor, partial_value, query_sum = carry
        scores = INV_TEMP * row_dot(query_bf, visitor)
        probs = jnp.exp(scores - log_total[:, None]).astype(jnp.bfloat16)
        query_sum = query_sum + jnp.dot(probs, visitor, preferred_element_type=jnp.float32)
        partial_value = partial_value + col_dot(probs, query_bf)
        visitor = shifted(visitor, "blk", 1)
        partial_value = shifted(partial_value, "blk", 1)
        return (visitor, partial_value, query_sum)

    empty = jnp.zeros((pair_count, width), jnp.float32)
    returned, item_sum, query_sum = lax.fori_loop(0, blocks, grad_hop, (item_bf, empty, empty))
    own = INV_TEMP * jnp.sum(query_bf.astype(jnp.float32) * item_bf.astype(jnp.float32), axis=1)
    loss = log_total - own
    query_unit_grad = INV_TEMP * (query_sum - item_bf.astype(jnp.float32))
    item_unit_grad = INV_TEMP * (item_sum - query_bf.astype(jnp.float32))
    item_grad = unit_backward(item_unit_grad, item_unit, item_scale)
    out_grad = unit_backward(query_unit_grad, query_unit, query_scale).astype(jnp.bfloat16)
    hidden_grad = (row_dot(out_grad, w_second) * silu_slope(hidden_pre)).astype(jnp.bfloat16)
    query_grad = row_dot(hidden_grad, w_first)
    return (loss, item_grad, query_grad)


def solution(mesh):
    placed = (P("table", None), P(), P(), P(("blk", "table"), None), P(("blk", "table"), None))
    return jax.shard_map(
        local,
        mesh=mesh,
        in_specs=placed,
        out_specs=(P(("blk", "table")), P(("blk", "table"), None), P(("blk", "table"), None)),
        check_vma=False,
    )
```

profile of v0, /device:TPU:8, one launch (start us, length us, event | category | flops | bytes accessed | tf_op | source)
XLA Modules:
  0.0 580.3 jit_solution(3756433420684838654)
XLA Ops:
  3.8 13.6 %reduce-window.6 = s32[48,16,128]{2,1,0:T(8,128)S(1)} reduce-window(s32[48,16,128]{2,1,0:T(8,128)S(1)} %fusion.12, s32[]{:T(128)} %constant.30.clone.1), window={size=1x1x128 pad=0_0x0_0x127_0}, to_apply=%region_0.0 | reduce-window | flops 12484608 | bytes 786436 | tf_op jit(solution)/shard_map/reduce-window
  26.6 30.8 %all_to_all.20 = s32[48,1,64]{2,1,0:T(1,128)S(1)} all-to-all(s32[48,1,64]{2,1,0:T(1,128)S(1)} %all_to_all.13), channel_id=1, replica_groups=mesh['blk'=16,'table'=48] {'table'}, dimensions={0} | all-to-all | bytes 24576 | tf_op jit(solution)/shard_map/all_to_all | solution.py:56
  57.5 14.8 %gather_fusion = bf16[3072,256]{1,0:T(8,128)(2,1)} fusion(bf16[8192,256]{1,0:T(8,128)(2,1)} %param.9, s32[3072]{0:T(1024)S(1)} %broadcast_clamp_fusion), kind=kCustom, calls=%fused_computation | custom fusion | bytes 3158016 | tf_op jit(solution)/shard_map/jit(_take)/gather | solution.py:55
  81.8 44.9 %all-to-all-done.1 = bf16[48,64,256]{2,1,0:T(8,128)(2,1)} async-done(((bf16[48,64,256]{2,1,0:T(8,128)(2,1)}), bf16[48,64,256]{2,1,0:T(8,128)(2,1)}, u32[]{:S(2)}, u32[]{:S(2)}) %all-to-all-start.1) | async-done | bytes 1572896 | tf_op jit(solution)/shard_map/all_to_all | solution.py:58
  141.3 187.1 %while.28 = (s32[]{:T(128)}, bf16[256,256]{1,0:T(8,128)(2,1)S(1)}, f32[256]{0:T(256)S(1)}, bf16[256,256]{1,0:T(8,128)(2,1)S(1)}, s32[]{:T(128)}, /*index=5*/s32[]{:T(128)}) while((s32[]{:T(128)}, bf16[256,256]{1,0:T(8,128)(2,1)S(1)}, f32[256]{0:T(256)S(1)}, bf16[256,256]{1,0:T(8,128)(2,1)S(1)}, s32[]{:T(128)}, ...), condition=%wide.region_10.11_spmd.clone, body=%wide.region_8.10_spmd.clone.sunk | while | flops 33685760 | bytes 1052791 | solution.py:79
  143.6 21.5 %collective-permute-done = bf16[256,256]{1,0:T(8,128)(2,1)S(1)} collective-permute-done((bf16[256,256]{1,0:T(8,128)(2,1)S(1)}, bf16[256,256]{1,0:T(8,128)(2,1)S(1)}, u32[]{:S(2)}, u32[]{:S(2)}) %collective-permute-start) | collective-permute-done | bytes 131104 | tf_op jit(solution)/shard_map/while/body/eval_jaxpr/ppermute | solution.py:12
  221.2 9.7 %collective-permute-done = bf16[256,256]{1,0:T(8,128)(2,1)S(1)} collective-permute-done((bf16[256,256]{1,0:T(8,128)(2,1)S(1)}, bf16[256,256]{1,0:T(8,128)(2,1)S(1)}, u32[]{:S(2)}, u32[]{:S(2)}) %collective-permute-start) | collective-permute-done | bytes 131104 | tf_op jit(solution)/shard_map/while/body/eval_jaxpr/ppermute | solution.py:12
  328.5 242.6 %while.29 = (s32[]{:T(128)}, bf16[256,256]{1,0:T(8,128)(2,1)S(1)}, f32[256,256]{1,0:T(8,128)S(1)}, f32[256,256]{1,0:T(8,128)S(1)}, bf16[256,256]{1,0:T(8,128)(2,...) while((s32[]{:T(128)}, bf16[256,256]{1,0:T(8,128)(2,1)S(1)}, f32[256,256]{1,0:T(8,128)S(1)}, ...), condition=%wide.region_13.14_spmd.clone, body=%wide.region_12.13_spmd.clone.sunk | while | flops 101056512 | bytes 3802287 | solution.py:95
  333.1 9.5 %collective-permute-done.1 = bf16[256,256]{1,0:T(8,128)(2,1)S(1)} collective-permute-done((bf16[256,256]{1,0:T(8,128)(2,1)S(1)}, bf16[256,256]{1,0:T(8,128)(2,1)S(1)}, u32[]{:S(2)}, u32[]{:S(2)}) %collective-permute-start.1) | collective-permute-done | bytes 131104 | tf_op jit(solution)/shard_map/while/body/eval_jaxpr/ppermute | solution.py:12
  347.2 9.5 %collective-permute-done.1 = bf16[256,256]{1,0:T(8,128)(2,1)S(1)} collective-permute-done((bf16[256,256]{1,0:T(8,128)(2,1)S(1)}, bf16[256,256]{1,0:T(8,128)(2,1)S(1)}, u32[]{:S(2)}, u32[]{:S(2)}) %collective-permute-start.1) | collective-permute-done | bytes 131104 | tf_op jit(solution)/shard_map/while/body/eval_jaxpr/ppermute | solution.py:12
  361.3 10.6 %collective-permute-done.1 = bf16[256,256]{1,0:T(8,128)(2,1)S(1)} collective-permute-done((bf16[256,256]{1,0:T(8,128)(2,1)S(1)}, bf16[256,256]{1,0:T(8,128)(2,1)S(1)}, u32[]{:S(2)}, u32[]{:S(2)}) %collective-permute-start.1) | collective-permute-done | bytes 131104 | tf_op jit(solution)/shard_map/while/body/eval_jaxpr/ppermute | solution.py:12
  376.4 11.7 %collective-permute-done.1 = bf16[256,256]{1,0:T(8,128)(2,1)S(1)} collective-permute-done((bf16[256,256]{1,0:T(8,128)(2,1)S(1)}, bf16[256,256]{1,0:T(8,128)(2,1)S(1)}, u32[]{:S(2)}, u32[]{:S(2)}) %collective-permute-start.1) | collective-permute-done | bytes 131104 | tf_op jit(solution)/shard_map/while/body/eval_jaxpr/ppermute | solution.py:12
  392.7 12.8 %collective-permute-done.1 = bf16[256,256]{1,0:T(8,128)(2,1)S(1)} collective-permute-done((bf16[256,256]{1,0:T(8,128)(2,1)S(1)}, bf16[256,256]{1,0:T(8,128)(2,1)S(1)}, u32[]{:S(2)}, u32[]{:S(2)}) %collective-permute-start.1) | collective-permute-done | bytes 131104 | tf_op jit(solution)/shard_map/while/body/eval_jaxpr/ppermute | solution.py:12
  410.1 13.4 %collective-permute-done.1 = bf16[256,256]{1,0:T(8,128)(2,1)S(1)} collective-permute-done((bf16[256,256]{1,0:T(8,128)(2,1)S(1)}, bf16[256,256]{1,0:T(8,128)(2,1)S(1)}, u32[]{:S(2)}, u32[]{:S(2)}) %collective-permute-start.1) | collective-permute-done | bytes 131104 | tf_op jit(solution)/shard_map/while/body/eval_jaxpr/ppermute | solution.py:12
  428.1 12.6 %collective-permute-done.1 = bf16[256,256]{1,0:T(8,128)(2,1)S(1)} collective-permute-done((bf16[256,256]{1,0:T(8,128)(2,1)S(1)}, bf16[256,256]{1,0:T(8,128)(2,1)S(1)}, u32[]{:S(2)}, u32[]{:S(2)}) %collective-permute-start.1) | collective-permute-done | bytes 131104 | tf_op jit(solution)/shard_map/while/body/eval_jaxpr/ppermute | solution.py:12
  445.2 11.7 %collective-permute-done.1 = bf16[256,256]{1,0:T(8,128)(2,1)S(1)} collective-permute-done((bf16[256,256]{1,0:T(8,128)(2,1)S(1)}, bf16[256,256]{1,0:T(8,128)(2,1)S(1)}, u32[]{:S(2)}, u32[]{:S(2)}) %collective-permute-start.1) | collective-permute-done | bytes 131104 | tf_op jit(solution)/shard_map/while/body/eval_jaxpr/ppermute | solution.py:12
  461.5 10.8 %collective-permute-done.1 = bf16[256,256]{1,0:T(8,128)(2,1)S(1)} collective-permute-done((bf16[256,256]{1,0:T(8,128)(2,1)S(1)}, bf16[256,256]{1,0:T(8,128)(2,1)S(1)}, u32[]{:S(2)}, u32[]{:S(2)}) %collective-permute-start.1) | collective-permute-done | bytes 131104 | tf_op jit(solution)/shard_map/while/body/eval_jaxpr/ppermute | solution.py:12
  476.8 9.8 %collective-permute-done.1 = bf16[256,256]{1,0:T(8,128)(2,1)S(1)} collective-permute-done((bf16[256,256]{1,0:T(8,128)(2,1)S(1)}, bf16[256,256]{1,0:T(8,128)(2,1)S(1)}, u32[]{:S(2)}, u32[]{:S(2)}) %collective-permute-start.1) | collective-permute-done | bytes 131104 | tf_op jit(solution)/shard_map/while/body/eval_jaxpr/ppermute | solution.py:12
  491.3 9.5 %collective-permute-done.1 = bf16[256,256]{1,0:T(8,128)(2,1)S(1)} collective-permute-done((bf16[256,256]{1,0:T(8,128)(2,1)S(1)}, bf16[256,256]{1,0:T(8,128)(2,1)S(1)}, u32[]{:S(2)}, u32[]{:S(2)}) %collective-permute-start.1) | collective-permute-done | bytes 131104 | tf_op jit(solution)/shard_map/while/body/eval_jaxpr/ppermute | solution.py:12
  505.3 9.5 %collective-permute-done.1 = bf16[256,256]{1,0:T(8,128)(2,1)S(1)} collective-permute-done((bf16[256,256]{1,0:T(8,128)(2,1)S(1)}, bf16[256,256]{1,0:T(8,128)(2,1)S(1)}, u32[]{:S(2)}, u32[]{:S(2)}) %collective-permute-start.1) | collective-permute-done | bytes 131104 | tf_op jit(solution)/shard_map/while/body/eval_jaxpr/ppermute | solution.py:12
  519.4 9.5 %collective-permute-done.1 = bf16[256,256]{1,0:T(8,128)(2,1)S(1)} collective-permute-done((bf16[256,256]{1,0:T(8,128)(2,1)S(1)}, bf16[256,256]{1,0:T(8,128)(2,1)S(1)}, u32[]{:S(2)}, u32[]{:S(2)}) %collective-permute-start.1) | collective-permute-done | bytes 131104 | tf_op jit(solution)/shard_map/while/body/eval_jaxpr/ppermute | solution.py:12
  533.5 9.5 %collective-permute-done.1 = bf16[256,256]{1,0:T(8,128)(2,1)S(1)} collective-permute-done((bf16[256,256]{1,0:T(8,128)(2,1)S(1)}, bf16[256,256]{1,0:T(8,128)(2,1)S(1)}, u32[]{:S(2)}, u32[]{:S(2)}) %collective-permute-start.1) | collective-permute-done | bytes 131104 | tf_op jit(solution)/shard_map/while/body/eval_jaxpr/ppermute | solution.py:12
  547.6 9.5 %collective-permute-done.1 = bf16[256,256]{1,0:T(8,128)(2,1)S(1)} collective-permute-done((bf16[256,256]{1,0:T(8,128)(2,1)S(1)}, bf16[256,256]{1,0:T(8,128)(2,1)S(1)}, u32[]{:S(2)}, u32[]{:S(2)}) %collective-permute-start.1) | collective-permute-done | bytes 131104 | tf_op jit(solution)/shard_map/while/body/eval_jaxpr/ppermute | solution.py:12
  561.6 9.5 %collective-permute-done.1 = bf16[256,256]{1,0:T(8,128)(2,1)S(1)} collective-permute-done((bf16[256,256]{1,0:T(8,128)(2,1)S(1)}, bf16[256,256]{1,0:T(8,128)(2,1)S(1)}, u32[]{:S(2)}, u32[]{:S(2)}) %collective-permute-start.1) | collective-permute-done | bytes 131104 | tf_op jit(solution)/shard_map/while/body/eval_jaxpr/ppermute | solution.py:12
  (262 shorter events, 273.7 us)
Async XLA Ops:
  74.9 51.8 %all-to-all-start.1 = ((bf16[48,64,256]{2,1,0:T(8,128)(2,1)}), bf16[48,64,256]{2,1,0:T(8,128)(2,1)}, u32[]{:S(2)}, u32[]{:S(2)}) async-start(bf16[48,64,256]{2,1,0:T(8,128)(2,1)} %broadcast_select_fusion), calls=%async_computation.1 | async-start | bytes 3145728 | tf_op jit(solution)/shard_map/all_to_all | solution.py:58
  141.4 23.7 %collective-permute-start = (bf16[256,256]{1,0:T(8,128)(2,1)S(1)}, bf16[256,256]{1,0:T(8,128)(2,1)S(1)}, u32[]{:S(2)}, u32[]{:S(2)}) collective-permute-start(bf16[256,256]{1,0:T(8,128)(2,1)S(1)} %copy.66), channel_id=1, source_target_pairs={{0,48},{48,96},{96,144},{144,192},{192,240},{240,288},{288,336},{3... | collective-permute-start | bytes 393224 | tf_op jit(solution)/shard_map/while/body/eval_jaxpr/ppermute | solution.py:12
  329.0 13.6 %collective-permute-start.2 = (f32[256,256]{1,0:T(8,128)S(1)}, f32[256,256]{1,0:T(8,128)S(1)}, u32[]{:S(2)}, u32[]{:S(2)}) collective-permute-start(f32[256,256]{1,0:T(8,128)S(1)} %convolution_add_fusion.4), channel_id=1, source_target_pairs={{0,48},{48,96},{96,144},{144,192},{192,240},{240,288},{288,336},{3... | collective-permute-start | bytes 786440 | tf_op jit(solution)/shard_map/while/body/eval_jaxpr/ppermute | solution.py:12
  343.1 13.6 %collective-permute-start.2 = (f32[256,256]{1,0:T(8,128)S(1)}, f32[256,256]{1,0:T(8,128)S(1)}, u32[]{:S(2)}, u32[]{:S(2)}) collective-permute-start(f32[256,256]{1,0:T(8,128)S(1)} %convolution_add_fusion.4), channel_id=1, source_target_pairs={{0,48},{48,96},{96,144},{144,192},{192,240},{240,288},{288,336},{3... | collective-permute-start | bytes 786440 | tf_op jit(solution)/shard_map/while/body/eval_jaxpr/ppermute | solution.py:12
  357.2 14.7 %collective-permute-start.2 = (f32[256,256]{1,0:T(8,128)S(1)}, f32[256,256]{1,0:T(8,128)S(1)}, u32[]{:S(2)}, u32[]{:S(2)}) collective-permute-start(f32[256,256]{1,0:T(8,128)S(1)} %convolution_add_fusion.4), channel_id=1, source_target_pairs={{0,48},{48,96},{96,144},{144,192},{192,240},{240,288},{288,336},{3... | collective-permute-start | bytes 786440 | tf_op jit(solution)/shard_map/while/body/eval_jaxpr/ppermute | solution.py:12
  372.3 15.8 %collective-permute-start.2 = (f32[256,256]{1,0:T(8,128)S(1)}, f32[256,256]{1,0:T(8,128)S(1)}, u32[]{:S(2)}, u32[]{:S(2)}) collective-permute-start(f32[256,256]{1,0:T(8,128)S(1)} %convolution_add_fusion.4), channel_id=1, source_target_pairs={{0,48},{48,96},{96,144},{144,192},{192,240},{240,288},{288,336},{3... | collective-permute-start | bytes 786440 | tf_op jit(solution)/shard_map/while/body/eval_jaxpr/ppermute | solution.py:12
  374.3 13.8 %collective-permute-start.1 = (bf16[256,256]{1,0:T(8,128)(2,1)S(1)}, bf16[256,256]{1,0:T(8,128)(2,1)S(1)}, u32[]{:S(2)}, u32[]{:S(2)}) collective-permute-start(bf16[256,256]{1,0:T(8,128)(2,1)S(1)} %copy.76), channel_id=1, source_target_pairs={{0,48},{48,96},{96,144},{144,192},{192,240},{240,288},{288,336},{3... | collective-permute-start | bytes 393224 | tf_op jit(solution)/shard_map/while/body/eval_jaxpr/ppermute | solution.py:12
  388.6 16.9 %collective-permute-start.2 = (f32[256,256]{1,0:T(8,128)S(1)}, f32[256,256]{1,0:T(8,128)S(1)}, u32[]{:S(2)}, u32[]{:S(2)}) collective-permute-start(f32[256,256]{1,0:T(8,128)S(1)} %convolution_add_fusion.4), channel_id=1, source_target_pairs={{0,48},{48,96},{96,144},{144,192},{192,240},{240,288},{288,336},{3... | collective-permute-start | bytes 786440 | tf_op jit(solution)/shard_map/while/body/eval_jaxpr/ppermute | solution.py:12
  390.5 15.0 %collective-permute-start.1 = (bf16[256,256]{1,0:T(8,128)(2,1)S(1)}, bf16[256,256]{1,0:T(8,128)(2,1)S(1)}, u32[]{:S(2)}, u32[]{:S(2)}) collective-permute-start(bf16[256,256]{1,0:T(8,128)(2,1)S(1)} %copy.76), channel_id=1, source_target_pairs={{0,48},{48,96},{96,144},{144,192},{192,240},{240,288},{288,336},{3... | collective-permute-start | bytes 393224 | tf_op jit(solution)/shard_map/while/body/eval_jaxpr/ppermute | solution.py:12
  406.0 17.5 %collective-permute-start.2 = (f32[256,256]{1,0:T(8,128)S(1)}, f32[256,256]{1,0:T(8,128)S(1)}, u32[]{:S(2)}, u32[]{:S(2)}) collective-permute-start(f32[256,256]{1,0:T(8,128)S(1)} %convolution_add_fusion.4), channel_id=1, source_target_pairs={{0,48},{48,96},{96,144},{144,192},{192,240},{240,288},{288,336},{3... | collective-permute-start | bytes 786440 | tf_op jit(solution)/shard_map/while/body/eval_jaxpr/ppermute | solution.py:12
  407.9 15.6 %collective-permute-start.1 = (bf16[256,256]{1,0:T(8,128)(2,1)S(1)}, bf16[256,256]{1,0:T(8,128)(2,1)S(1)}, u32[]{:S(2)}, u32[]{:S(2)}) collective-permute-start(bf16[256,256]{1,0:T(8,128)(2,1)S(1)} %copy.76), channel_id=1, source_target_pairs={{0,48},{48,96},{96,144},{144,192},{192,240},{240,288},{288,336},{3... | collective-permute-start | bytes 393224 | tf_op jit(solution)/shard_map/while/body/eval_jaxpr/ppermute | solution.py:12
  424.0 16.7 %collective-permute-start.2 = (f32[256,256]{1,0:T(8,128)S(1)}, f32[256,256]{1,0:T(8,128)S(1)}, u32[]{:S(2)}, u32[]{:S(2)}) collective-permute-start(f32[256,256]{1,0:T(8,128)S(1)} %convolution_add_fusion.4), channel_id=1, source_target_pairs={{0,48},{48,96},{96,144},{144,192},{192,240},{240,288},{288,336},{3... | collective-permute-start | bytes 786440 | tf_op jit(solution)/shard_map/while/body/eval_jaxpr/ppermute | solution.py:12
  425.9 14.7 %collective-permute-start.1 = (bf16[256,256]{1,0:T(8,128)(2,1)S(1)}, bf16[256,256]{1,0:T(8,128)(2,1)S(1)}, u32[]{:S(2)}, u32[]{:S(2)}) collective-permute-start(bf16[256,256]{1,0:T(8,128)(2,1)S(1)} %copy.76), channel_id=1, source_target_pairs={{0,48},{48,96},{96,144},{144,192},{192,240},{240,288},{288,336},{3... | collective-permute-start | bytes 393224 | tf_op jit(solution)/shard_map/while/body/eval_jaxpr/ppermute | solution.py:12
  441.1 15.8 %collective-permute-start.2 = (f32[256,256]{1,0:T(8,128)S(1)}, f32[256,256]{1,0:T(8,128)S(1)}, u32[]{:S(2)}, u32[]{:S(2)}) collective-permute-start(f32[256,256]{1,0:T(8,128)S(1)} %convolution_add_fusion.4), channel_id=1, source_target_pairs={{0,48},{48,96},{96,144},{144,192},{192,240},{240,288},{288,336},{3... | collective-permute-start | bytes 786440 | tf_op jit(solution)/shard_map/while/body/eval_jaxpr/ppermute | solution.py:12
  443.1 13.8 %collective-permute-start.1 = (bf16[256,256]{1,0:T(8,128)(2,1)S(1)}, bf16[256,256]{1,0:T(8,128)(2,1)S(1)}, u32[]{:S(2)}, u32[]{:S(2)}) collective-permute-start(bf16[256,256]{1,0:T(8,128)(2,1)S(1)} %copy.76), channel_id=1, source_target_pairs={{0,48},{48,96},{96,144},{144,192},{192,240},{240,288},{288,336},{3... | collective-permute-start | bytes 393224 | tf_op jit(solution)/shard_map/while/body/eval_jaxpr/ppermute | solution.py:12
  457.4 14.9 %collective-permute-start.2 = (f32[256,256]{1,0:T(8,128)S(1)}, f32[256,256]{1,0:T(8,128)S(1)}, u32[]{:S(2)}, u32[]{:S(2)}) collective-permute-start(f32[256,256]{1,0:T(8,128)S(1)} %convolution_add_fusion.4), channel_id=1, source_target_pairs={{0,48},{48,96},{96,144},{144,192},{192,240},{240,288},{288,336},{3... | collective-permute-start | bytes 786440 | tf_op jit(solution)/shard_map/while/body/eval_jaxpr/ppermute | solution.py:12
  459.3 12.9 %collective-permute-start.1 = (bf16[256,256]{1,0:T(8,128)(2,1)S(1)}, bf16[256,256]{1,0:T(8,128)(2,1)S(1)}, u32[]{:S(2)}, u32[]{:S(2)}) collective-permute-start(bf16[256,256]{1,0:T(8,128)(2,1)S(1)} %copy.76), channel_id=1, source_target_pairs={{0,48},{48,96},{96,144},{144,192},{192,240},{240,288},{288,336},{3... | collective-permute-start | bytes 393224 | tf_op jit(solution)/shard_map/while/body/eval_jaxpr/ppermute | solution.py:12
  472.8 13.9 %collective-permute-start.2 = (f32[256,256]{1,0:T(8,128)S(1)}, f32[256,256]{1,0:T(8,128)S(1)}, u32[]{:S(2)}, u32[]{:S(2)}) collective-permute-start(f32[256,256]{1,0:T(8,128)S(1)} %convolution_add_fusion.4), channel_id=1, source_target_pairs={{0,48},{48,96},{96,144},{144,192},{192,240},{240,288},{288,336},{3... | collective-permute-start | bytes 786440 | tf_op jit(solution)/shard_map/while/body/eval_jaxpr/ppermute | solution.py:12
  487.2 13.6 %collective-permute-start.2 = (f32[256,256]{1,0:T(8,128)S(1)}, f32[256,256]{1,0:T(8,128)S(1)}, u32[]{:S(2)}, u32[]{:S(2)}) collective-permute-start(f32[256,256]{1,0:T(8,128)S(1)} %convolution_add_fusion.4), channel_id=1, source_target_pairs={{0,48},{48,96},{96,144},{144,192},{192,240},{240,288},{288,336},{3... | collective-permute-start | bytes 786440 | tf_op jit(solution)/shard_map/while/body/eval_jaxpr/ppermute | solution.py:12
  501.2 13.6 %collective-permute-start.2 = (f32[256,256]{1,0:T(8,128)S(1)}, f32[256,256]{1,0:T(8,128)S(1)}, u32[]{:S(2)}, u32[]{:S(2)}) collective-permute-start(f32[256,256]{1,0:T(8,128)S(1)} %convolution_add_fusion.4), channel_id=1, source_target_pairs={{0,48},{48,96},{96,144},{144,192},{192,240},{240,288},{288,336},{3... | collective-permute-start | bytes 786440 | tf_op jit(solution)/shard_map/while/body/eval_jaxpr/ppermute | solution.py:12
  515.3 13.6 %collective-permute-start.2 = (f32[256,256]{1,0:T(8,128)S(1)}, f32[256,256]{1,0:T(8,128)S(1)}, u32[]{:S(2)}, u32[]{:S(2)}) collective-permute-start(f32[256,256]{1,0:T(8,128)S(1)} %convolution_add_fusion.4), channel_id=1, source_target_pairs={{0,48},{48,96},{96,144},{144,192},{192,240},{240,288},{288,336},{3... | collective-permute-start | bytes 786440 | tf_op jit(solution)/shard_map/while/body/eval_jaxpr/ppermute | solution.py:12
  529.4 13.6 %collective-permute-start.2 = (f32[256,256]{1,0:T(8,128)S(1)}, f32[256,256]{1,0:T(8,128)S(1)}, u32[]{:S(2)}, u32[]{:S(2)}) collective-permute-start(f32[256,256]{1,0:T(8,128)S(1)} %convolution_add_fusion.4), channel_id=1, source_target_pairs={{0,48},{48,96},{96,144},{144,192},{192,240},{240,288},{288,336},{3... | collective-permute-start | bytes 786440 | tf_op jit(solution)/shard_map/while/body/eval_jaxpr/ppermute | solution.py:12
  543.5 13.6 %collective-permute-start.2 = (f32[256,256]{1,0:T(8,128)S(1)}, f32[256,256]{1,0:T(8,128)S(1)}, u32[]{:S(2)}, u32[]{:S(2)}) collective-permute-start(f32[256,256]{1,0:T(8,128)S(1)} %convolution_add_fusion.4), channel_id=1, source_target_pairs={{0,48},{48,96},{96,144},{144,192},{192,240},{240,288},{288,336},{3... | collective-permute-start | bytes 786440 | tf_op jit(solution)/shard_map/while/body/eval_jaxpr/ppermute | solution.py:12
  557.5 13.6 %collective-permute-start.2 = (f32[256,256]{1,0:T(8,128)S(1)}, f32[256,256]{1,0:T(8,128)S(1)}, u32[]{:S(2)}, u32[]{:S(2)}) collective-permute-start(f32[256,256]{1,0:T(8,128)S(1)} %convolution_add_fusion.4), channel_id=1, source_target_pairs={{0,48},{48,96},{96,144},{144,192},{192,240},{240,288},{288,336},{3... | collective-permute-start | bytes 786440 | tf_op jit(solution)/shard_map/while/body/eval_jaxpr/ppermute | solution.py:12
  (35 other events, 441.3 us)
where the time goes:
time: 582 us; the launch traced here: 580 us
  waiting for transfers between devices  366 us (63%)
  starting transfers between devices  98.7 us (17%)
  local copies, waits for them, and re-layouts  38.8 us (7%)
  blocking collectives  30.8 us (5%)
  matrix products  22.6 us (4%)
  other arithmetic  21.6 us (4%)
    ppermute x48, waiting for transfers between devices, shifted(): lax.ppermute(shard, axis, [(i, (i + by) % count) for i in range(count)])  321 us
    ppermute x48, starting transfers between devices, shifted(): lax.ppermute(shard, axis, [(i, (i + by) % count) for i in range(count)])  92.2 us
    all_to_all x1, waiting for transfers between devices, local(): lax.all_to_all(found, 'table', split_axis=0, concat_axis=0, tiled=True)  44.9 us
    all_to_all x1, blocking collectives, local(): lax.all_to_all(requests, 'table', split_axis=0, concat_axis=0, tiled=True)  30.8 us
    gather x1, local copies, waits for them, and re-layouts, local(): jnp.take(id_table, lax.all_to_all(requests, 'table', split_axis=0, concat...  14.8 us
    another operation x3, other arithmetic  14 us
    dot_general x33, matrix products, row_dot(): lax.dot_general(left, right, (((1,), (1,)), ((), ())), preferred_element_...  13.4 us
  transfers between devices with their start and end apart: 49, of which 33 were waited for; matrix products, arithmetic and copies ran while one was open for 1% of the time, Pallas kernels for 0%

commit v1 on v0

v1 whole, which is shorter than its diff:
```python
import functools
import math

import jax
import jax.numpy as jnp
from jax import lax
from jax.experimental import pallas as pl
from jax.experimental.pallas import tpu as pltpu
from jax.sharding import PartitionSpec as P

EPS = 1e-06
INV_TEMP = 20.0
MESH = pl.DeviceIdType.MESH
F32 = jnp.float32
BF16 = jnp.bfloat16


def row_dot(left, right):
    return lax.dot_general(left, right, (((1,), (1,)), ((), ())), preferred_element_type=F32)


def col_dot(left, right):
    return lax.dot_general(left, right, (((0,), (0,)), ((), ())), preferred_element_type=F32)


def dot(left, right):
    return jnp.dot(left, right, preferred_element_type=F32)


def unit_rows(vectors):
    scale = lax.rsqrt(jnp.sum(vectors * vectors, axis=-1, keepdims=True) + EPS)
    return vectors * scale, scale


def unit_backward(grad, unit, scale):
    return scale * (grad - unit * jnp.sum(unit * grad, axis=-1, keepdims=True))


def lookup_kernel(
    n, cap, owner_ref, row_ref, table_ref, query_ref, item_ref,
    table_bf, table_wide, req_all, req_out, req_in, req_smem, rows_out, rows_in, select, stage, total,
    local_sem, req_send, req_recv, rows_send, rows_recv,
):
    me = lax.axis_index("table")
    pairs, bags = owner_ref.shape
    shard_rows = table_ref.shape[0]
    step_rows = stage.shape[0]
    chunks, _, chunk = select.shape

    fetch = pltpu.make_async_copy(table_ref, table_bf, local_sem.at[0])
    fetch.start()
    barrier = pltpu.get_barrier_semaphore()

    def greet(step, _):
        peer = lax.rem(me + step, n)
        pl.semaphore_signal(barrier, inc=1, device_id={"table": peer}, device_id_type=MESH)
        return 0

    lax.fori_loop(1, n, greet, 0)

    lanes = req_all.shape[0]
    wide = 2 * cap
    shard_lane = lax.broadcasted_iota(jnp.int32, (pairs, lanes), 1)
    slot_lane = lax.broadcasted_iota(jnp.int32, (pairs, wide), 1)
    upper_half = slot_lane >= cap
    slot_of_lane = jnp.where(upper_half, slot_lane - cap, slot_lane)
    earlier = jnp.where(
        lax.broadcasted_iota(jnp.int32, (pairs, pairs), 0)
        > lax.broadcasted_iota(jnp.int32, (pairs, pairs), 1),
        1.0, 0.0,
    ).astype(BF16)
    counts = jnp.zeros((1, lanes), F32)
    wanted = jnp.zeros((lanes, wide), F32)
    places = []
    for k in range(bags):
        owner = owner_ref[:, k : k + 1]
        row = row_ref[:, k : k + 1]
        hot = jnp.where(owner == shard_lane, 1.0, 0.0)
        hot_bf = hot.astype(BF16)
        before = dot(earlier, hot_bf) + counts
        slot = jnp.sum(hot * before, axis=1, keepdims=True).astype(jnp.int32)
        counts = counts + jnp.sum(hot, axis=0, keepdims=True)
        digit = jnp.where(upper_half, row & 127, row >> 7).astype(F32)
        digit = jnp.where(slot_of_lane == slot, digit, 0.0).astype(BF16)
        wanted = wanted + col_dot(hot_bf, digit)
        places.append(owner * cap + slot)
    wanted = wanted * 128.0 + pltpu.roll(wanted, cap, 1)
    req_all[...] = wanted.astype(jnp.int32)

    def split(shard, _):
        req_out[shard] = req_all[pl.ds(shard, 1), :]
        return 0

    lax.fori_loop(0, n, split, 0)
    req_in[me] = req_out[me]
    pl.semaphore_wait(barrier, n - 1)

    def request(peer):
        return pltpu.make_async_remote_copy(
            src_ref=req_out.at[peer], dst_ref=req_in.at[me],
            send_sem=req_send.at[peer], recv_sem=req_recv.at[me],
            device_id={"table": peer}, device_id_type=MESH,
        )

    def ask(step, _):
        request(lax.rem(me + step, n)).start()
        return 0

    lax.fori_loop(1, n, ask, 0)

    fetch.wait()
    blocks = 32
    block_rows = shard_rows // blocks

    def widen(block, _):
        at = pl.ds(pl.multiple_of(block * block_rows, block_rows), block_rows)
        table_wide[at, :] = table_bf[at, :].astype(F32)
        return 0

    lax.fori_loop(0, blocks, widen, 0)

    half = bags // 2

    def choose(block, _):
        column = lax.broadcasted_iota(jnp.int32, (pairs, chunk), 1) + block * chunk
        for side in range(2):
            mask = places[side * half] == column
            for k in range(side * half + 1, (side + 1) * half):
                mask = mask | (places[k] == column)
            select[block, side * pairs : (side + 1) * pairs, :] = jnp.where(mask, 1.0, 0.0).astype(BF16)
        return 0

    lax.fori_loop(0, chunks, choose, 0)

    def asked(step, _):
        peer = lax.rem(me + step, n)
        pltpu.make_async_remote_copy(
            src_ref=req_out.at[peer], dst_ref=req_in.at[peer],
            send_sem=req_send.at[peer], recv_sem=req_recv.at[peer],
            device_id={"table": peer}, device_id_type=MESH,
        ).wait()
        return 0

    lax.fori_loop(1, n, asked, 0)
    to_smem = pltpu.make_async_copy(req_in, req_smem, local_sem.at[1])
    to_smem.start()
    to_smem.wait()

    def gather(peer, target, start):
        def some(part, _):
            for s in range(step_rows):
                index = req_smem[peer, 0, part * step_rows + s] & (shard_rows - 1)
                stage[s : s + 1, :] = table_wide[pl.ds(index, 1), :]
            at = pl.multiple_of(start + part * step_rows, step_rows)
            target[pl.ds(at, step_rows), :] = stage[...].astype(BF16)
            return 0

        lax.fori_loop(0, cap // step_rows, some, 0)

    def sending(peer, slot):
        return pltpu.make_async_remote_copy(
            src_ref=rows_out.at[pl.ds(pl.multiple_of(peer * cap, cap), cap), :],
            dst_ref=rows_in.at[pl.ds(pl.multiple_of(slot * cap, cap), cap), :],
            send_sem=rows_send.at[peer], recv_sem=rows_recv.at[slot],
            device_id={"table": peer}, device_id_type=MESH,
        )

    def serve(step, _):
        away = n // 2 - (step + 1) // 2
        offset = away + (step % 2) * (n - 2 * away)
        peer = lax.rem(me + offset, n)
        gather(peer, rows_out, peer * cap)
        sending(peer, me).start()
        return 0

    lax.fori_loop(0, n - 1, serve, 0)
    gather(me, rows_in, me * cap)

    total[...] = jnp.zeros_like(total)

    def arrived(source, _):
        @pl.when(source != me)
        def _():
            sending(source, source).wait()

        return 0

    def combine(block, _):
        each = chunk // cap
        lax.fori_loop(block * each, (block + 1) * each, arrived, 0)
        at = pl.ds(pl.multiple_of(block * chunk, chunk), chunk)
        total[...] += dot(select[block], rows_in[at, :])
        return 0

    lax.fori_loop(0, chunks, combine, 0)
    query_ref[...] = total[0:pairs, :].astype(BF16)
    item_ref[...] = total[pairs : 2 * pairs, :]


def lookup(n, id_table, owner_ids, row_ids):
    pairs, bags = owner_ids.shape
    width = id_table.shape[1]
    cap = min(pairs, 3 * pairs * bags // (2 * n))
    lanes = max(128, n)
    slots = n * cap
    chunk = min(slots, 8 * cap)
    vmem = pl.BlockSpec(memory_space=pltpu.VMEM)
    return pl.pallas_call(
        functools.partial(lookup_kernel, n, cap),
        out_shape=(
            jax.ShapeDtypeStruct((pairs, width), BF16),
            jax.ShapeDtypeStruct((pairs, width), F32),
        ),
        in_specs=[vmem, vmem, pl.BlockSpec(memory_space=pl.ANY)],
        out_specs=(vmem, vmem),
        scratch_shapes=[
            pltpu.VMEM(id_table.shape, BF16),
            pltpu.VMEM(id_table.shape, F32),
            pltpu.VMEM((lanes, 2 * cap), jnp.int32),
            pltpu.VMEM((n, 1, 2 * cap), jnp.int32),
            pltpu.VMEM((n, 1, 2 * cap), jnp.int32),
            pltpu.SMEM((n, 1, 2 * cap), jnp.int32),
            pltpu.VMEM((slots, width), BF16),
            pltpu.VMEM((slots, width), BF16),
            pltpu.VMEM((slots // chunk, 2 * pairs, chunk), BF16),
            pltpu.VMEM((16, width), F32),
            pltpu.VMEM((2 * pairs, width), F32),
            pltpu.SemaphoreType.DMA((2,)),
            pltpu.SemaphoreType.DMA((n,)),
            pltpu.SemaphoreType.DMA((n,)),
            pltpu.SemaphoreType.DMA((n,)),
            pltpu.SemaphoreType.DMA((n,)),
        ],
        compiler_params=pltpu.CompilerParams(
            collective_id=0, has_side_effects=True, vmem_limit_bytes=48 * 2**20
        ),
        name="lookup",
    )(owner_ids, row_ids, id_table)


def train_kernel(
    nx, nz, query_ref, item_ref, first_hbm, second_hbm, loss_ref, item_grad_ref, query_grad_ref,
    first, second, slope, items, queries, exps, total_out, total_in,
    query_out, query_in, item_sum, item_out, item_in, acc,
    local_sem, send_sem, recv_sem,
):
    blk = lax.axis_index("blk")
    x, z = blk // nz, blk % nz
    pairs, width = query_ref.shape
    steps, chunk = slope.shape[0], slope.shape[2]

    load_first = pltpu.make_async_copy(first_hbm, first, local_sem.at[0])
    load_second = pltpu.make_async_copy(second_hbm, second, local_sem.at[1])
    load_first.start()
    load_second.start()

    def along_x(step):
        there = lax.rem(x + step, nx)
        return there, there * nz + z

    def along_z(step):
        there = lax.rem(z + step, nz)
        return there, x * nz + there

    barrier = pltpu.get_barrier_semaphore()
    for axis, count in ((along_x, nx), (along_z, nz)):
        for step in range(1, count):
            pl.semaphore_signal(
                barrier, inc=1, device_id={"blk": axis(step)[1]}, device_id_type=MESH
            )

    item_unit, item_scale = unit_rows(item_ref[...])
    items[z] = item_unit.astype(BF16)
    pl.semaphore_wait(barrier, nx + nz - 2)

    def copy(phase, source, target, landing, step, axis):
        there, device = axis(step)
        return pltpu.make_async_remote_copy(
            src_ref=source, dst_ref=target,
            send_sem=send_sem.at[phase, there], recv_sem=recv_sem.at[phase, landing],
            device_id={"blk": device}, device_id_type=MESH,
        )

    def item_copy(step, slot):
        return copy(0, items.at[z], items.at[slot], slot, step, along_z)

    def query_copy(step, slot):
        return copy(1, queries.at[x], queries.at[slot], slot, step, along_x)

    def total_copy(step, slot):
        return copy(2, total_out, total_in.at[slot], slot, step, along_x)

    def query_sum_copy(step, slot):
        there = along_x(step)[0]
        return copy(3, query_out.at[there], query_in.at[slot], slot, step, along_x)

    def item_sum_copy(step, slot):
        there = along_z(step)[0]
        return copy(4, item_out.at[there], item_in.at[slot], slot, step, along_z)

    for step in range(1, nz):
        item_copy(step, z).start()

    acc[...] = jnp.zeros_like(acc)
    load_first.wait()
    load_second.wait()

    def forward(part, _):
        at = pl.ds(pl.multiple_of(part * chunk, chunk), chunk)
        pre = dot(query_ref[...], first[:, at])
        sigma = 0.5 + 0.5 * jnp.tanh(0.5 * pre)
        slope[part] = sigma * (1.0 + pre * (1.0 - sigma))
        acc[...] += dot((pre * sigma).astype(BF16), second[at, :])
        return 0

    lax.fori_loop(0, steps, forward, 0)
    query_unit, query_scale = unit_rows(acc[...])
    queries[x] = query_unit.astype(BF16)
    for step in range(1, nx):
        query_copy(step, x).start()

    diagonal = lax.broadcasted_iota(jnp.int32, (pairs, pairs), 0) == lax.broadcasted_iota(
        jnp.int32, (pairs, pairs), 1
    )

    own = None
    for step in range(nx):
        xi = along_x(step)[0]
        if step > 0:
            query_copy(step, xi).wait_recv()
        part = jnp.zeros((1, pairs), F32)
        for turn in range(nz):
            zi = along_z(turn)[0]
            if step == 0 and turn > 0:
                item_copy(turn, zi).wait_recv()
            scores = INV_TEMP * row_dot(items[zi], queries[xi])
            if step == 0 and turn == 0:
                own = jnp.sum(jnp.where(diagonal, scores, 0.0), axis=0, keepdims=True)
            value = jnp.exp(scores)
            exps[step, zi] = value
            part = part + jnp.sum(value, axis=0, keepdims=True)
        total_out[xi] = part
    total_in[x] = total_out[...]
    for step in range(1, nx):
        total_copy(step, x).start()
    for step in range(1, nx):
        total_copy(step, along_x(step)[0]).wait_recv()

    all_items = items[...].reshape(nz * pairs, width)
    query_sum = None
    for turn in range(nx):
        step = (turn + 1) % nx
        xi = along_x(step)[0]
        total = jnp.zeros((1, pairs), F32)
        for source in range(nx):
            total = total + total_in[source, xi]
        if step == 0:
            loss_ref[...] = jnp.log(total) - own
        prob = (exps[step].reshape(nz * pairs, pairs) * (1.0 / total)).astype(BF16)
        part = col_dot(prob, all_items)
        if step == 0:
            query_sum = part
        else:
            query_out[xi] = part.astype(BF16)
            query_sum_copy(step, x).start()
        added = dot(prob, queries[xi]).reshape(nz, pairs, width)
        item_sum[...] = added if turn == 0 else item_sum[...] + added
    for step in range(1, nz):
        zi = along_z(step)[0]
        item_out[zi] = item_sum[zi].astype(BF16)
        item_sum_copy(step, z).start()

    for step in range(1, nx):
        xi = along_x(step)[0]
        query_sum_copy(step, xi).wait_recv()
        query_sum = query_sum + query_in[xi].astype(F32)
    query_unit_grad = INV_TEMP * (query_sum - items[z].astype(F32))
    query_unit = acc[...] * query_scale
    out_grad = unit_backward(query_unit_grad, query_unit, query_scale).astype(BF16)
    acc[...] = jnp.zeros_like(acc)

    def backward(part, _):
        at = pl.ds(pl.multiple_of(part * chunk, chunk), chunk)
        hidden_grad = (row_dot(out_grad, second[at, :]) * slope[part]).astype(BF16)
        acc[...] += row_dot(hidden_grad, first[:, at])
        return 0

    lax.fori_loop(0, steps, backward, 0)
    query_grad_ref[...] = acc[...]

    total_items = item_sum[z]
    for step in range(1, nz):
        zi = along_z(step)[0]
        item_sum_copy(step, zi).wait_recv()
        total_items = total_items + item_in[zi].astype(F32)
    item_unit_grad = INV_TEMP * (total_items - queries[x].astype(F32))
    item_unit, item_scale = unit_rows(item_ref[...])
    item_grad_ref[...] = unit_backward(item_unit_grad, item_unit, item_scale)

    for step in range(1, nz):
        item_copy(step, z).wait_send()
        item_sum_copy(step, z).wait_send()
    for step in range(1, nx):
        query_copy(step, x).wait_send()
        total_copy(step, x).wait_send()
        query_sum_copy(step, x).wait_send()


def train(nx, nz, query_in, item_in, w_first, w_second):
    pairs, width = query_in.shape
    hidden = w_first.shape[1]
    chunk = min(hidden, 512)
    vmem = pl.BlockSpec(memory_space=pltpu.VMEM)
    hbm = pl.BlockSpec(memory_space=pl.ANY)
    most = max(nx, nz)
    return pl.pallas_call(
        functools.partial(train_kernel, nx, nz),
        out_shape=(
            jax.ShapeDtypeStruct((1, pairs), F32),
            jax.ShapeDtypeStruct((pairs, width), F32),
            jax.ShapeDtypeStruct((pairs, width), F32),
        ),
        in_specs=[vmem, vmem, hbm, hbm],
        out_specs=(vmem, vmem, vmem),
        scratch_shapes=[
            pltpu.VMEM(w_first.shape, BF16),
            pltpu.VMEM(w_second.shape, BF16),
            pltpu.VMEM((hidden // chunk, pairs, chunk), F32),
            pltpu.VMEM((nz, pairs, width), BF16),
            pltpu.VMEM((nx, pairs, width), BF16),
            pltpu.VMEM((nx, nz, pairs, pairs), F32),
            pltpu.VMEM((nx, 1, pairs), F32),
            pltpu.VMEM((nx, nx, 1, pairs), F32),
            pltpu.VMEM((nx, pairs, width), BF16),
            pltpu.VMEM((nx, pairs, width), BF16),
            pltpu.VMEM((nz, pairs, width), F32),
            pltpu.VMEM((nz, pairs, width), BF16),
            pltpu.VMEM((nz, pairs, width), BF16),
            pltpu.VMEM((pairs, width), F32),
            pltpu.SemaphoreType.DMA((2,)),
            pltpu.SemaphoreType.DMA((5, most)),
            pltpu.SemaphoreType.DMA((5, most)),
        ],
        compiler_params=pltpu.CompilerParams(
            collective_id=1, has_side_effects=True, vmem_limit_bytes=48 * 2**20
        ),
        name="train",
    )(query_in, item_in, w_first, w_second)


def local(nx, nz, n, id_table, w_first, w_second, owner_ids, row_ids):
    query_in, item_in = lookup(n, id_table, owner_ids, row_ids)
    loss, item_grad, query_grad = train(nx, nz, query_in, item_in, w_first, w_second)
    return loss.reshape(-1), item_grad, query_grad


def solution(mesh):
    blocks, shards = mesh.shape["blk"], mesh.shape["table"]
    nx = math.isqrt(blocks)
    nz = blocks // nx
    placed = (P("table", None), P(), P(), P(("blk", "table"), None), P(("blk", "table"), None))
    return jax.shard_map(
        functools.partial(local, nx, nz, shards),
        mesh=mesh,
        in_specs=placed,
        out_specs=(P(("blk", "table")), P(("blk", "table"), None), P(("blk", "table"), None)),
        check_vma=False,
    )
```

time: 582 us -> 148 us (0.25)
  the two profiles are of different devices: /device:TPU:8 before, /device:TPU:104 now
where the time goes in v1:
time: 148 us
  Pallas kernels  141 us (95%)
  local copies, waits for them, and re-layouts  5.8 us (4%)
    pallas_call x1, Pallas kernels, lookup(): pl.pallas_call(functools.partial(lookup_kernel, n, cap), out_shape=(jax.S...  95.6 us
    pallas_call x1, Pallas kernels, train(): pl.pallas_call(functools.partial(train_kernel, nx, nz), out_shape=(jax.Sh...  45.5 us
    unnamed x11, local copies, waits for them, and re-layouts  5.8 us

profile of v1, /device:TPU:104, one launch (start us, length us, event | category | flops | bytes accessed | tf_op | source)
XLA Modules:
  0.0 147.6 jit_solution(4139717389351891515)
XLA Ops:
  0.6 0.8 copy.8.owner_ref
  1.5 0.8 copy.9.row_ref
  2.3 0.0 copy-start
  2.3 2.2 %copy-done = bf16[8192,256]{1,0:T(8,128)(2,1)S(1)} copy-done((bf16[8192,256]{1,0:T(8,128)(2,1)S(1)}, bf16[8192,256]{1,0:T(8,128)(2,1)}, u32[]{:S(2)}) %copy-start) | copy-done | bytes 4194328
  4.5 0.0 copy-start.1
  4.5 0.0 copy-start.2
  4.5 95.6 %lookup.1 = (bf16[256,256]{1,0:T(8,128)(2,1)S(1)}, f32[256,256]{1,0:T(8,128)S(1)}) custom-call(s32[256,8]{1,0:T(8,128)S(1)} %copy.8.owner_ref, s32[256,8]{1,0:T(8,128)S(1)} %copy.9.row_ref, bf16[8192,256]{1,0:T(8,128)(2,1)S(1)} %copy-done), custom_call_target="tpu_custom_call" | custom-call | tf_op jit(solution)/shard_map/lookup/pallas_call | solution.py:208
  100.1 0.0 copy-done.1
  100.1 0.0 copy-done.2
  100.1 45.5 %train.1 = (f32[1,256]{1,0:T(1,128)S(1)}, f32[256,256]{1,0:T(8,128)S(1)}, f32[256,256]{1,0:T(8,128)S(1)}) custom-call(bf16[256,256]{1,0:T(8,128)(2,1)S(1)} %get-tuple-element.8.query_ref, f32[256,256]{1,0:T(8,128)S(1)} %get-tuple-element.9.item_ref, bf16[256,4096]{1,0:T(8,128)(2,1)S(1)} %copy-done.1, bf16[4096,256]{1,0:T(8,128)(2,1)S(1)} %copy-done.2), custom_call_target="tpu_custom_call" | custom-call | tf_op jit(solution)/shard_map/train/pallas_call | solution.py:416
  145.6 0.6 copy.13
  146.2 0.7 copy.14
  146.9 0.7 copy.15
Async XLA Ops:
  2.3 2.2 %copy-start = (bf16[8192,256]{1,0:T(8,128)(2,1)S(1)}, bf16[8192,256]{1,0:T(8,128)(2,1)}, u32[]{:S(2)}) copy-start(bf16[8192,256]{1,0:T(8,128)(2,1)} %table_ref.1) | copy-start | bytes 12582916
  4.5 95.6 %copy-start.1 = (bf16[256,4096]{1,0:T(8,128)(2,1)S(1)}, bf16[256,4096]{1,0:T(8,128)(2,1)}, u32[]{:S(2)}) copy-start(bf16[256,4096]{1,0:T(8,128)(2,1)} %first_hbm.1) | copy-start | bytes 6291460
  4.5 95.6 %copy-start.2 = (bf16[4096,256]{1,0:T(8,128)(2,1)S(1)}, bf16[4096,256]{1,0:T(8,128)(2,1)}, u32[]{:S(2)}) copy-start(bf16[4096,256]{1,0:T(8,128)(2,1)} %second_hbm.1) | copy-start | bytes 6291460

commit v2 on v1

v2 whole, which is shorter than its diff:
```python
import functools
import math

import jax
import jax.numpy as jnp
from jax import lax
from jax.experimental import pallas as pl
from jax.experimental.pallas import tpu as pltpu
from jax.sharding import PartitionSpec as P

EPS = 1e-06
INV_TEMP = 20.0
MESH = pl.DeviceIdType.MESH
F32 = jnp.float32
BF16 = jnp.bfloat16


def row_dot(left, right):
    return lax.dot_general(left, right, (((1,), (1,)), ((), ())), preferred_element_type=F32)


def col_dot(left, right):
    return lax.dot_general(left, right, (((0,), (0,)), ((), ())), preferred_element_type=F32)


def dot(left, right):
    return jnp.dot(left, right, preferred_element_type=F32)


def unit_rows(vectors):
    scale = lax.rsqrt(jnp.sum(vectors * vectors, axis=-1, keepdims=True) + EPS)
    return vectors * scale, scale


def unit_backward(grad, unit, scale):
    return scale * (grad - unit * jnp.sum(unit * grad, axis=-1, keepdims=True))


def lookup(grid, meet, owner_ref, row_ref, table_ref, query_ref, item_ref, refs):
    ny, planes, cores = grid
    (table_bf, table_wide, ids, code_rows, codes, req_out, req_in, req_smem, rows_out, rows_in, select,
     stage, part_out, part_in, local_sem, ids_send, ids_recv, req_send, req_recv, rows_send, rows_recv,
     part_send, part_recv) = refs
    bags, pairs = owner_ref.shape
    shard_rows, width = table_ref.shape
    cap, half_width = rows_in.shape[3:]
    chunks, chunk = select.shape[1], select.shape[3]
    step_rows = stage.shape[0]
    half = bags // 2
    m = ny * cores
    t = lax.axis_index("table")
    plane = (t // cores) % planes
    q = t // (planes * cores) * cores + t % cores

    def shard(place, where):
        return place // cores * (planes * cores) + where * cores + place % cores

    def column(r):
        return {"table": shard(q, lax.rem(plane + r, planes))}

    def across(place):
        return {"table": shard(place, plane)}

    def around(step):
        away = m // 2 - (step + 1) // 2
        return lax.rem(q + away + (step % 2) * (m - 2 * away), m)

    fetch = pltpu.make_async_copy(table_ref, table_bf, local_sem.at[0])
    fetch.start()
    barrier = pltpu.get_barrier_semaphore()

    def greet(step, _):
        pl.semaphore_signal(barrier, inc=1, device_id=across(around(step)), device_id_type=MESH)
        return 0

    lax.fori_loop(0, m - 1, greet, 0)
    for r in range(1, planes):
        pl.semaphore_signal(barrier, inc=1, device_id=column(r), device_id_type=MESH)
    others = meet(barrier)
    ids[0] = owner_ref[...] * shard_rows + row_ref[...]
    code_rows[...] = jnp.zeros_like(code_rows)
    pl.semaphore_wait(barrier, m - 1 + planes - 1 + others)

    def ids_copy(r, slot):
        return pltpu.make_async_remote_copy(
            src_ref=ids.at[0], dst_ref=ids.at[slot], send_sem=ids_send.at[r], recv_sem=ids_recv.at[slot],
            device_id=column(r), device_id_type=MESH,
        )

    for r in range(1, planes):
        ids_copy(r, planes - r).start()

    place_iota = lax.broadcasted_iota(jnp.int32, (m, pairs), 0)
    plane_shards = place_iota + place_iota // cores * (planes * cores - cores) + plane * cores
    first_slot = (place_iota * cap).astype(F32)
    digit_iota = lax.broadcasted_iota(jnp.int32, (2 * cap, pairs), 0)
    low_digit = digit_iota >= cap
    digit_slot = jnp.where(low_digit, digit_iota - cap, digit_iota).astype(F32)
    earlier = jnp.where(
        lax.broadcasted_iota(jnp.int32, (pairs, pairs), 0)
        < lax.broadcasted_iota(jnp.int32, (pairs, pairs), 1),
        1.0, 0.0,
    ).astype(BF16)
    bits = shard_rows.bit_length() - 1

    def route(r):
        packed = ids[r]
        owner, row = packed >> bits, packed & (shard_rows - 1)
        hots = [jnp.where(owner[k : k + 1, :] == plane_shards, 1.0, 0.0) for k in range(bags)]
        before = dot(jnp.concatenate(hots, axis=0).astype(BF16), earlier)
        count = jnp.zeros((m, 1), F32)
        digits = []
        for k in range(bags):
            hot = hots[k]
            held = before[k * m : (k + 1) * m, :] + count
            inside = jnp.sum(hot, axis=0, keepdims=True)
            slot = jnp.sum(hot * held, axis=0, keepdims=True)
            code = slot + jnp.sum(hot * first_slot, axis=0, keepdims=True)
            code_rows[k : k + 1, :] = jnp.where(inside > 0.0, code, -1.0)
            digit = jnp.where(low_digit, row[k : k + 1, :] & 127, row[k : k + 1, :] >> 7).astype(F32)
            digits.append(jnp.where(digit_slot == slot, digit, 0.0).astype(BF16))
            count = count + jnp.sum(hot, axis=1, keepdims=True)
        hot_all = jnp.concatenate([hot.astype(BF16) for hot in hots], axis=1)
        wanted = row_dot(hot_all, jnp.concatenate(digits, axis=1))
        wanted = (wanted * 128.0 + pltpu.roll(wanted, cap, 1)).astype(jnp.int32)
        for place in range(m):
            req_out[place, r : r + 1, :] = wanted[place : place + 1, :]
        codes[r] = jnp.transpose(code_rows[...]).astype(jnp.int32)

    route(0)
    fetch.wait()
    blocks = 32
    block_rows = shard_rows // blocks

    def widen(block, _):
        at = pl.ds(pl.multiple_of(block * block_rows, block_rows), block_rows)
        table_wide[at, :] = table_bf[at, :].astype(F32)
        return 0

    lax.fori_loop(0, blocks, widen, 0)
    for r in range(1, planes):
        ids_copy(r, r).wait()
        route(r)

    def request(place, slot):
        return pltpu.make_async_remote_copy(
            src_ref=req_out.at[place], dst_ref=req_in.at[slot],
            send_sem=req_send.at[place], recv_sem=req_recv.at[slot],
            device_id=across(place), device_id_type=MESH,
        )

    def ask(step, _):
        request(around(step), q).start()
        return 0

    lax.fori_loop(0, m - 1, ask, 0)
    req_in[q] = req_out[q]

    def choose(r):
        def some(block, _):
            place = lax.broadcasted_iota(jnp.int32, (pairs, chunk), 1) + block * chunk
            for side in range(2):
                mask = codes[r, :, side * half : side * half + 1] == place
                for k in range(side * half + 1, (side + 1) * half):
                    mask = mask | (codes[r, :, k : k + 1] == place)
                select[r, block, side * pairs : (side + 1) * pairs, :] = jnp.where(mask, 1.0, 0.0).astype(BF16)
            return 0

        lax.fori_loop(0, chunks, some, 0)

    for r in range(1, planes):
        choose(r)

    def asked(step, _):
        place = around(step)
        request(place, place).wait()
        return 0

    lax.fori_loop(0, m - 1, asked, 0)
    to_smem = pltpu.make_async_copy(req_in, req_smem, local_sem.at[1])
    to_smem.start()
    to_smem.wait()

    def gather(place, r, left, right):
        def some(part, _):
            for s in range(step_rows):
                index = req_smem[place, r, part * step_rows + s] & (shard_rows - 1)
                stage[s : s + 1, :] = table_wide[pl.ds(index, 1), :]
            at = pl.ds(pl.multiple_of(part * step_rows, step_rows), step_rows)
            rows = stage[...].astype(BF16)
            left[at, :] = rows[:, :half_width]
            right[at, :] = rows[:, half_width:]
            return 0

        lax.fori_loop(0, cap // step_rows, some, 0)

    foreign = pl.ds(1, planes - 1)

    def foreign_copy(side, place, slot):
        return pltpu.make_async_remote_copy(
            src_ref=rows_out.at[side, place, foreign], dst_ref=rows_in.at[side, foreign, slot],
            send_sem=rows_send.at[side, place], recv_sem=rows_recv.at[side, slot],
            device_id=across(place), device_id_type=MESH,
        )

    def near_copy(place, slot):
        return pltpu.make_async_remote_copy(
            src_ref=rows_out.at[:, place, 0], dst_ref=rows_in.at[:, 0, slot],
            send_sem=rows_send.at[2, place], recv_sem=rows_recv.at[2, slot],
            device_id=across(place), device_id_type=MESH,
        )

    def serve_foreign(step, _):
        place = around(step)
        for r in range(1, planes):
            gather(place, r, rows_out.at[0, place, r], rows_out.at[1, place, r])
        foreign_copy(0, place, q).start()
        return 0

    def serve_second(step, _):
        foreign_copy(1, around(step), q).start()
        return 0

    def serve_near(step, _):
        place = around(step)
        gather(place, 0, rows_out.at[0, place, 0], rows_out.at[1, place, 0])
        near_copy(place, q).start()
        return 0

    lax.fori_loop(0, m - 1, serve_foreign, 0)
    lax.fori_loop(0, m - 1, serve_second, 0)
    lax.fori_loop(0, m - 1, serve_near, 0)
    for r in range(planes):
        gather(q, r, rows_in.at[0, r, q], rows_in.at[1, r, q])

    def bag_sums(side, r):
        rows = rows_in[side, r].reshape(m * cap, half_width)
        total = dot(select[r, 0], rows[:chunk])
        for block in range(1, chunks):
            total = total + dot(select[r, block], rows[block * chunk : (block + 1) * chunk])
        return total

    def part_copy(side, r, slot):
        return pltpu.make_async_remote_copy(
            src_ref=part_out.at[side, r], dst_ref=part_in.at[side, slot],
            send_sem=part_send.at[side, r], recv_sem=part_recv.at[side, slot],
            device_id=column(r), device_id_type=MESH,
        )

    for side in range(2):
        def foreign_here(step, _):
            place = around(step)
            foreign_copy(side, place, place).wait()
            return 0

        lax.fori_loop(0, m - 1, foreign_here, 0)
        for r in range(1, planes):
            part_out[side, r] = bag_sums(side, r).astype(BF16)
            part_copy(side, r, planes - r).start()

    choose(0)

    def near_here(step, _):
        place = around(step)
        near_copy(place, place).wait()
        return 0

    lax.fori_loop(0, m - 1, near_here, 0)
    for side in range(2):
        total = bag_sums(side, 0)
        for r in range(1, planes):
            part_copy(side, r, r).wait()
            total = total + part_in[side, r].astype(F32)
        columns = slice(side * half_width, (side + 1) * half_width)
        query_ref[:, columns] = total[:pairs].astype(BF16)
        item_ref[:, columns] = total[pairs:]


def lookup_scratch(grid, bags, pairs, table):
    ny, planes, cores = grid
    shard_rows, width = table.shape
    m = ny * cores
    cap = min(pairs, 3 * pairs * bags // (2 * m * planes))
    chunk = min(m * cap, 512)
    dma = pltpu.SemaphoreType.DMA
    return [
        pltpu.VMEM(table.shape, BF16),
        pltpu.VMEM(table.shape, F32),
        pltpu.VMEM((planes, bags, pairs), jnp.int32),
        pltpu.VMEM((128, pairs), F32),
        pltpu.VMEM((planes, pairs, 128), jnp.int32),
        pltpu.VMEM((m, planes, 2 * cap), jnp.int32),
        pltpu.VMEM((m, planes, 2 * cap), jnp.int32),
        pltpu.SMEM((m, planes, 2 * cap), jnp.int32),
        pltpu.VMEM((2, m, planes, cap, width // 2), BF16),
        pltpu.VMEM((2, planes, m, cap, width // 2), BF16),
        pltpu.VMEM((planes, m * cap // chunk, 2 * pairs, chunk), BF16),
        pltpu.VMEM((16, width), F32),
        pltpu.VMEM((2, planes, 2 * pairs, width // 2), BF16),
        pltpu.VMEM((2, planes, 2 * pairs, width // 2), BF16),
        dma((2,)),
        dma((planes,)),
        dma((planes,)),
        dma((m,)),
        dma((m,)),
        dma((3, m)),
        dma((3, m)),
        dma((2, planes)),
        dma((2, planes)),
    ]


def kernel(
    grid, nx, nz, owner_ref, row_ref, table_hbm, first_hbm, second_hbm, loss_ref, item_grad_ref, query_grad_ref,
    query_ref, item_ref, first, second, slope, items, queries, exps, total_out, total_in,
    query_out, query_in, item_sum, item_out, item_in, acc,
    local_sem, send_sem, recv_sem, *lookup_refs,
):
    blk = lax.axis_index("blk")
    x, z = blk // nz, blk % nz
    pairs, width = query_ref.shape
    steps, chunk = slope.shape[0], slope.shape[2]

    load_first = pltpu.make_async_copy(first_hbm, first, local_sem.at[0])
    load_second = pltpu.make_async_copy(second_hbm, second, local_sem.at[1])
    load_first.start()
    load_second.start()

    def along_x(step):
        there = lax.rem(x + step, nx)
        return there, there * nz + z

    def along_z(step):
        there = lax.rem(z + step, nz)
        return there, x * nz + there

    def meet(barrier):
        for axis, count in ((along_x, nx), (along_z, nz)):
            for step in range(1, count):
                pl.semaphore_signal(
                    barrier, inc=1, device_id={"blk": axis(step)[1]}, device_id_type=MESH
                )
        return nx + nz - 2

    lookup(grid, meet, owner_ref, row_ref, table_hbm, query_ref, item_ref, lookup_refs)
    item_unit, item_scale = unit_rows(item_ref[...])
    items[z] = item_unit.astype(BF16)

    def copy(phase, source, target, landing, step, axis):
        there, device = axis(step)
        return pltpu.make_async_remote_copy(
            src_ref=source, dst_ref=target,
            send_sem=send_sem.at[phase, there], recv_sem=recv_sem.at[phase, landing],
            device_id={"blk": device}, device_id_type=MESH,
        )

    def item_copy(step, slot):
        return copy(0, items.at[z], items.at[slot], slot, step, along_z)

    def query_copy(step, slot):
        return copy(1, queries.at[x], queries.at[slot], slot, step, along_x)

    def total_copy(step, slot):
        return copy(2, total_out, total_in.at[slot], slot, step, along_x)

    def query_sum_copy(step, slot):
        there = along_x(step)[0]
        return copy(3, query_out.at[there], query_in.at[slot], slot, step, along_x)

    def item_sum_copy(step, slot):
        there = along_z(step)[0]
        return copy(4, item_out.at[there], item_in.at[slot], slot, step, along_z)

    for step in range(1, nz):
        item_copy(step, z).start()

    acc[...] = jnp.zeros_like(acc)
    load_first.wait()
    load_second.wait()

    def forward(part, _):
        at = pl.ds(pl.multiple_of(part * chunk, chunk), chunk)
        pre = dot(query_ref[...], first[:, at])
        sigma = 0.5 + 0.5 * jnp.tanh(0.5 * pre)
        slope[part] = sigma * (1.0 + pre * (1.0 - sigma))
        acc[...] += dot((pre * sigma).astype(BF16), second[at, :])
        return 0

    lax.fori_loop(0, steps, forward, 0)
    query_unit, query_scale = unit_rows(acc[...])
    queries[x] = query_unit.astype(BF16)
    for step in range(1, nx):
        query_copy(step, x).start()

    diagonal = lax.broadcasted_iota(jnp.int32, (pairs, pairs), 0) == lax.broadcasted_iota(
        jnp.int32, (pairs, pairs), 1
    )

    own = None
    for step in range(nx):
        xi = along_x(step)[0]
        if step > 0:
            query_copy(step, xi).wait_recv()
        part = jnp.zeros((1, pairs), F32)
        for turn in range(nz):
            zi = along_z(turn)[0]
            if step == 0 and turn > 0:
                item_copy(turn, zi).wait_recv()
            scores = INV_TEMP * row_dot(items[zi], queries[xi])
            if step == 0 and turn == 0:
                own = jnp.sum(jnp.where(diagonal, scores, 0.0), axis=0, keepdims=True)
            value = jnp.exp(scores)
            exps[step, zi] = value
            part = part + jnp.sum(value, axis=0, keepdims=True)
        total_out[xi] = part
    total_in[x] = total_out[...]
    for step in range(1, nx):
        total_copy(step, x).start()
    for step in range(1, nx):
        total_copy(step, along_x(step)[0]).wait_recv()

    all_items = items[...].reshape(nz * pairs, width)
    query_sum = None
    for turn in range(nx):
        step = (turn + 1) % nx
        xi = along_x(step)[0]
        total = jnp.zeros((1, pairs), F32)
        for source in range(nx):
            total = total + total_in[source, xi]
        if step == 0:
            loss_ref[...] = jnp.log(total) - own
        prob = (exps[step].reshape(nz * pairs, pairs) * (1.0 / total)).astype(BF16)
        part = col_dot(prob, all_items)
        if step == 0:
            query_sum = part
        else:
            query_out[xi] = part.astype(BF16)
            query_sum_copy(step, x).start()
        added = dot(prob, queries[xi]).reshape(nz, pairs, width)
        item_sum[...] = added if turn == 0 else item_sum[...] + added
    for step in range(1, nz):
        zi = along_z(step)[0]
        item_out[zi] = item_sum[zi].astype(BF16)
        item_sum_copy(step, z).start()

    for step in range(1, nx):
        xi = along_x(step)[0]
        query_sum_copy(step, xi).wait_recv()
        query_sum = query_sum + query_in[xi].astype(F32)
    query_unit_grad = INV_TEMP * (query_sum - items[z].astype(F32))
    query_unit = acc[...] * query_scale
    out_grad = unit_backward(query_unit_grad, query_unit, query_scale).astype(BF16)
    acc[...] = jnp.zeros_like(acc)

    def backward(part, _):
        at = pl.ds(pl.multiple_of(part * chunk, chunk), chunk)
        hidden_grad = (row_dot(out_grad, second[at, :]) * slope[part]).astype(BF16)
        acc[...] += row_dot(hidden_grad, first[:, at])
        return 0

    lax.fori_loop(0, steps, backward, 0)
    query_grad_ref[...] = acc[...]

    total_items = item_sum[z]
    for step in range(1, nz):
        zi = along_z(step)[0]
        item_sum_copy(step, zi).wait_recv()
        total_items = total_items + item_in[zi].astype(F32)
    item_unit_grad = INV_TEMP * (total_items - queries[x].astype(F32))
    item_unit, item_scale = unit_rows(item_ref[...])
    item_grad_ref[...] = unit_backward(item_unit_grad, item_unit, item_scale)

    for step in range(1, nz):
        item_copy(step, z).wait_send()
        item_sum_copy(step, z).wait_send()
    for step in range(1, nx):
        query_copy(step, x).wait_send()
        total_copy(step, x).wait_send()
        query_sum_copy(step, x).wait_send()


def local(grid, nx, nz, id_table, w_first, w_second, owner_ids, row_ids):
    pairs, bags = owner_ids.shape
    width, hidden = w_first.shape
    chunk = min(hidden, 512)
    vmem = pl.BlockSpec(memory_space=pltpu.VMEM)
    hbm = pl.BlockSpec(memory_space=pltpu.HBM)
    most = max(nx, nz)
    loss, item_grad, query_grad = pl.pallas_call(
        functools.partial(kernel, grid, nx, nz),
        out_shape=(
            jax.ShapeDtypeStruct((1, pairs), F32),
            jax.ShapeDtypeStruct((pairs, width), F32),
            jax.ShapeDtypeStruct((pairs, width), F32),
        ),
        in_specs=[vmem, vmem, hbm, hbm, hbm],
        out_specs=(vmem, vmem, vmem),
        scratch_shapes=[
            pltpu.VMEM((pairs, width), BF16),
            pltpu.VMEM((pairs, width), F32),
            pltpu.VMEM(w_first.shape, BF16),
            pltpu.VMEM(w_second.shape, BF16),
            pltpu.VMEM((hidden // chunk, pairs, chunk), F32),
            pltpu.VMEM((nz, pairs, width), BF16),
            pltpu.VMEM((nx, pairs, width), BF16),
            pltpu.VMEM((nx, nz, pairs, pairs), F32),
            pltpu.VMEM((nx, 1, pairs), F32),
            pltpu.VMEM((nx, nx, 1, pairs), F32),
            pltpu.VMEM((nx, pairs, width), BF16),
            pltpu.VMEM((nx, pairs, width), BF16),
            pltpu.VMEM((nz, pairs, width), F32),
            pltpu.VMEM((nz, pairs, width), BF16),
            pltpu.VMEM((nz, pairs, width), BF16),
            pltpu.VMEM((pairs, width), F32),
            pltpu.SemaphoreType.DMA((2,)),
            pltpu.SemaphoreType.DMA((5, most)),
            pltpu.SemaphoreType.DMA((5, most)),
            *lookup_scratch(grid, bags, pairs, id_table),
        ],
        compiler_params=pltpu.CompilerParams(
            collective_id=0, has_side_effects=True, vmem_limit_bytes=60 * 2**20
        ),
        name="step",
    )(owner_ids.T, row_ids.T, id_table, w_first, w_second)
    return loss.reshape(-1), item_grad, query_grad


def solution(mesh):
    blocks, shards = mesh.shape["blk"], mesh.shape["table"]
    nx = math.isqrt(blocks)
    nz = blocks // nx
    grid = (shards // 6, 3, 2)
    placed = (P("table", None), P(), P(), P(("blk", "table"), None), P(("blk", "table"), None))
    return jax.shard_map(
        functools.partial(local, grid, nx, nz),
        mesh=mesh,
        in_specs=placed,
        out_specs=(P(("blk", "table")), P(("blk", "table"), None), P(("blk", "table"), None)),
        check_vma=False,
    )
```

time: 148 us -> 112 us (0.76)
  the two profiles are of different devices: /device:TPU:104 before, /device:TPU:8 now
where the time goes in v2:
time: 112 us; the launch traced here: 111 us
  Pallas kernels  106 us (95%)
  local copies, waits for them, and re-layouts  4.54 us (4%)
    pallas_call x1, Pallas kernels, local(): pl.pallas_call(functools.partial(kernel, grid, nx, nz), out_shape=(jax.Sh...  106 us
    unnamed x3, local copies, waits for them, and re-layouts  4.54 us

profile of v2, /device:TPU:8, one launch (start us, length us, event | category | flops | bytes accessed | tf_op | source)
XLA Modules:
  0.0 111.3 jit_solution(15282708774927642845)
XLA Ops:
  0.6 106.1 %step.1 = (f32[1,256]{1,0:T(1,128)}, f32[256,256]{1,0:T(8,128)}, f32[256,256]{1,0:T(8,128)}) custom-call(s32[8,256]{1,0:T(8,128)} %bitcast.3, s32[8,256]{1,0:T(8,128)} %bitcast.4, bf16[8192,256]{1,0:T(8,128)(2,1)} %table_hbm.1, bf16[256,4096]{1,0:T(8,128)(2,1)} %first_hbm.1, bf16[4096,256]{1,0:T(8,128)(2,1)} %second_hbm.1), custom_call_target="tpu_custom_call" | custom-call | tf_op jit(solution)/shard_map/step/pallas_call | solution.py:489
  106.8 1.2 %copy.11 = f32[256]{0:T(256)} copy(f32[256]{0:T(256)} %bitcast.5) | data formatting | bytes 2048
  108.0 1.7 %copy.12 = f32[256,256]{1,0:T(8,128)} copy(f32[256,256]{1,0:T(8,128)} %get-tuple-element.13) | data formatting | bytes 524288
  109.6 1.7 %copy.13 = f32[256,256]{1,0:T(8,128)} copy(f32[256,256]{1,0:T(8,128)} %get-tuple-element.14) | data formatting | bytes 524288

commit v3 on v2

--- a/solution.py
+++ b/solution.py
@@ -36,9 +36,9 @@
     return scale * (grad - unit * jnp.sum(unit * grad, axis=-1, keepdims=True))
 
 
-def lookup(grid, meet, owner_ref, row_ref, table_ref, query_ref, item_ref, refs):
+def lookup(grid, meet, owner_ref, row_ref, table_ref, refs):
     ny, planes, cores = grid
-    (table_bf, table_wide, ids, code_rows, codes, req_out, req_in, req_smem, rows_out, rows_in, select,
+    (table_bf, table_wide, ids, code_rows, codes, req_all, req_out, req_in, req_smem, rows_out, rows_in, select,
      stage, part_out, part_in, local_sem, ids_send, ids_recv, req_send, req_recv, rows_send, rows_recv,
      part_send, part_recv) = refs
     bags, pairs = owner_ref.shape
@@ -48,6 +48,7 @@
     step_rows = stage.shape[0]
     half = bags // 2
     m = ny * cores
+    n = m * planes
     t = lax.axis_index("table")
     plane = (t // cores) % planes
     q = t // (planes * cores) * cores + t % cores
@@ -65,34 +66,23 @@
         away = m // 2 - (step + 1) // 2
         return lax.rem(q + away + (step % 2) * (m - 2 * away), m)
 
+    def further(step):
+        return lax.rem(t + step, n)
+
     fetch = pltpu.make_async_copy(table_ref, table_bf, local_sem.at[0])
     fetch.start()
     barrier = pltpu.get_barrier_semaphore()
 
     def greet(step, _):
-        pl.semaphore_signal(barrier, inc=1, device_id=across(around(step)), device_id_type=MESH)
-        return 0
-
-    lax.fori_loop(0, m - 1, greet, 0)
-    for r in range(1, planes):
-        pl.semaphore_signal(barrier, inc=1, device_id=column(r), device_id_type=MESH)
+        pl.semaphore_signal(barrier, inc=1, device_id={"table": further(step)}, device_id_type=MESH)
+        return 0
+
+    lax.fori_loop(1, n, greet, 0)
     others = meet(barrier)
-    ids[0] = owner_ref[...] * shard_rows + row_ref[...]
-    code_rows[...] = jnp.zeros_like(code_rows)
-    pl.semaphore_wait(barrier, m - 1 + planes - 1 + others)
-
-    def ids_copy(r, slot):
-        return pltpu.make_async_remote_copy(
-            src_ref=ids.at[0], dst_ref=ids.at[slot], send_sem=ids_send.at[r], recv_sem=ids_recv.at[slot],
-            device_id=column(r), device_id_type=MESH,
-        )
-
-    for r in range(1, planes):
-        ids_copy(r, planes - r).start()
-
-    place_iota = lax.broadcasted_iota(jnp.int32, (m, pairs), 0)
-    plane_shards = place_iota + place_iota // cores * (planes * cores - cores) + plane * cores
-    first_slot = (place_iota * cap).astype(F32)
+
+    shard_iota = lax.broadcasted_iota(jnp.int32, (n, pairs), 0)
+    shard_place = shard_iota // (planes * cores) * cores + shard_iota % cores
+    first_slot = ((shard_iota // cores % planes * m + shard_place) * cap).astype(F32)
     digit_iota = lax.broadcasted_iota(jnp.int32, (2 * cap, pairs), 0)
     low_digit = digit_iota >= cap
     digit_slot = jnp.where(low_digit, digit_iota - cap, digit_iota).astype(F32)
@@ -101,33 +91,52 @@
         < lax.broadcasted_iota(jnp.int32, (pairs, pairs), 1),
         1.0, 0.0,
     ).astype(BF16)
-    bits = shard_rows.bit_length() - 1
-
-    def route(r):
-        packed = ids[r]
-        owner, row = packed >> bits, packed & (shard_rows - 1)
-        hots = [jnp.where(owner[k : k + 1, :] == plane_shards, 1.0, 0.0) for k in range(bags)]
-        before = dot(jnp.concatenate(hots, axis=0).astype(BF16), earlier)
-        count = jnp.zeros((m, 1), F32)
-        digits = []
-        for k in range(bags):
-            hot = hots[k]
-            held = before[k * m : (k + 1) * m, :] + count
-            inside = jnp.sum(hot, axis=0, keepdims=True)
-            slot = jnp.sum(hot * held, axis=0, keepdims=True)
-            code = slot + jnp.sum(hot * first_slot, axis=0, keepdims=True)
-            code_rows[k : k + 1, :] = jnp.where(inside > 0.0, code, -1.0)
-            digit = jnp.where(low_digit, row[k : k + 1, :] & 127, row[k : k + 1, :] >> 7).astype(F32)
-            digits.append(jnp.where(digit_slot == slot, digit, 0.0).astype(BF16))
-            count = count + jnp.sum(hot, axis=1, keepdims=True)
-        hot_all = jnp.concatenate([hot.astype(BF16) for hot in hots], axis=1)
-        wanted = row_dot(hot_all, jnp.concatenate(digits, axis=1))
-        wanted = (wanted * 128.0 + pltpu.roll(wanted, cap, 1)).astype(jnp.int32)
-        for place in range(m):
-            req_out[place, r : r + 1, :] = wanted[place : place + 1, :]
-        codes[r] = jnp.transpose(code_rows[...]).astype(jnp.int32)
-
-    route(0)
+    count = jnp.zeros((n, 1), F32)
+    wanted = jnp.zeros((n, 2 * cap), F32)
+    for k in range(bags):
+        hot = jnp.where(owner_ref[k : k + 1, :] == shard_iota, 1.0, 0.0)
+        hot_bf = hot.astype(BF16)
+        held = dot(hot_bf, earlier) + count
+        slot = jnp.sum(hot * held, axis=0, keepdims=True)
+        code = slot + jnp.sum(hot * first_slot, axis=0, keepdims=True)
+        ids[0, k : k + 1, :] = code.astype(jnp.int32)
+        row = row_ref[k : k + 1, :]
+        digit = jnp.where(low_digit, row & 127, row >> 7).astype(F32)
+        digit = jnp.where(digit_slot == slot, digit, 0.0).astype(BF16)
+        wanted = wanted + row_dot(hot_bf, digit)
+        count = count + jnp.sum(hot, axis=1, keepdims=True)
+    req_all[...] = (wanted * 128.0 + pltpu.roll(wanted, cap, 1)).astype(jnp.int32)
+
+    def split(place, _):
+        req_out[place] = req_all[pl.ds(place, 1), :]
+        return 0
+
+    lax.fori_loop(0, n, split, 0)
+    req_in[t] = req_out[t]
+    pl.semaphore_wait(barrier, n - 1 + others)
+
+    def request(to, slot):
+        return pltpu.make_async_remote_copy(
+            src_ref=req_out.at[to], dst_ref=req_in.at[slot],
+            send_sem=req_send.at[to], recv_sem=req_recv.at[slot],
+            device_id={"table": to}, device_id_type=MESH,
+        )
+
+    def ask(step, _):
+        request(further(step), t).start()
+        return 0
+
+    lax.fori_loop(1, n, ask, 0)
+
+    def ids_copy(r, slot):
+        return pltpu.make_async_remote_copy(
+            src_ref=ids.at[0], dst_ref=ids.at[slot], send_sem=ids_send.at[r], recv_sem=ids_recv.at[slot],
+            device_id=column(r), device_id_type=MESH,
+        )
+
+    for r in range(1, planes):
+        ids_copy(r, planes - r).start()
+
     fetch.wait()
     blocks = 32
     block_rows = shard_rows // blocks
@@ -138,53 +147,22 @@
         return 0
 
     lax.fori_loop(0, blocks, widen, 0)
-    for r in range(1, planes):
-        ids_copy(r, r).wait()
-        route(r)
-
-    def request(place, slot):
-        return pltpu.make_async_remote_copy(
-            src_ref=req_out.at[place], dst_ref=req_in.at[slot],
-            send_sem=req_send.at[place], recv_sem=req_recv.at[slot],
-            device_id=across(place), device_id_type=MESH,
-        )
-
-    def ask(step, _):
-        request(around(step), q).start()
-        return 0
-
-    lax.fori_loop(0, m - 1, ask, 0)
-    req_in[q] = req_out[q]
-
-    def choose(r):
-        def some(block, _):
-            place = lax.broadcasted_iota(jnp.int32, (pairs, chunk), 1) + block * chunk
-            for side in range(2):
-                mask = codes[r, :, side * half : side * half + 1] == place
-                for k in range(side * half + 1, (side + 1) * half):
-                    mask = mask | (codes[r, :, k : k + 1] == place)
-                select[r, block, side * pairs : (side + 1) * pairs, :] = jnp.where(mask, 1.0, 0.0).astype(BF16)
-            return 0
-
-        lax.fori_loop(0, chunks, some, 0)
-
-    for r in range(1, planes):
-        choose(r)
 
     def asked(step, _):
-        place = around(step)
-        request(place, place).wait()
-        return 0
-
-    lax.fori_loop(0, m - 1, asked, 0)
+        request(further(step), further(step)).wait()
+        return 0
+
+    lax.fori_loop(1, n, asked, 0)
     to_smem = pltpu.make_async_copy(req_in, req_smem, local_sem.at[1])
     to_smem.start()
     to_smem.wait()
 
     def gather(place, r, left, right):
+        asker = shard(place, lax.rem(plane + r, planes))
+
         def some(part, _):
             for s in range(step_rows):
-                index = req_smem[place, r, part * step_rows + s] & (shard_rows - 1)
+                index = req_smem[asker, 0, part * step_rows + s] & (shard_rows - 1)
                 stage[s : s + 1, :] = table_wide[pl.ds(index, 1), :]
             at = pl.ds(pl.multiple_of(part * step_rows, step_rows), step_rows)
             rows = stage[...].astype(BF16)
@@ -221,29 +199,54 @@
         foreign_copy(1, around(step), q).start()
         return 0
 
-    def serve_near(step, _):
+    def collect_near(step, _):
         place = around(step)
         gather(place, 0, rows_out.at[0, place, 0], rows_out.at[1, place, 0])
-        near_copy(place, q).start()
+        return 0
+
+    def serve_near(step, _):
+        near_copy(around(step), q).start()
         return 0
 
     lax.fori_loop(0, m - 1, serve_foreign, 0)
     lax.fori_loop(0, m - 1, serve_second, 0)
-    lax.fori_loop(0, m - 1, serve_near, 0)
     for r in range(planes):
         gather(q, r, rows_in.at[0, r, q], rows_in.at[1, r, q])
-
-    def bag_sums(side, r):
+    lax.fori_loop(0, m - 1, collect_near, 0)
+
+    code_rows[...] = jnp.zeros_like(code_rows)
+
+    def choose(r):
+        code_rows[0:bags, :] = ids[r].astype(F32)
+        codes[...] = jnp.transpose(code_rows[...]).astype(jnp.int32) - plane * (m * cap)
+
+        def some(block, _):
+            place = lax.broadcasted_iota(jnp.int32, (pairs, chunk), 1) + block * chunk
+            for side in range(2):
+                mask = codes[:, side * half : side * half + 1] == place
+                for k in range(side * half + 1, (side + 1) * half):
+                    mask = mask | (codes[:, k : k + 1] == place)
+                select[r, block, side * pairs : (side + 1) * pairs, :] = jnp.where(mask, 1.0, 0.0).astype(BF16)
+            return 0
+
+        lax.fori_loop(0, chunks, some, 0)
+
+    for r in range(1, planes):
+        ids_copy(r, r).wait()
+        choose(r)
+
+    def bag_sums(side, r, bag):
         rows = rows_in[side, r].reshape(m * cap, half_width)
-        total = dot(select[r, 0], rows[:chunk])
+        at = slice(bag * pairs, (bag + 1) * pairs)
+        total = dot(select[r, 0, at, :], rows[:chunk])
         for block in range(1, chunks):
-            total = total + dot(select[r, block], rows[block * chunk : (block + 1) * chunk])
+            total = total + dot(select[r, block, at, :], rows[block * chunk : (block + 1) * chunk])
         return total
 
-    def part_copy(side, r, slot):
+    def part_copy(side, r, bag, slot):
         return pltpu.make_async_remote_copy(
-            src_ref=part_out.at[side, r], dst_ref=part_in.at[side, slot],
-            send_sem=part_send.at[side, r], recv_sem=part_recv.at[side, slot],
+            src_ref=part_out.at[side, r, bag], dst_ref=part_in.at[side, slot, bag],
+            send_sem=part_send.at[side, r, bag], recv_sem=part_recv.at[side, slot, bag],
             device_id=column(r), device_id_type=MESH,
         )
 
@@ -254,9 +257,12 @@
             return 0
 
         lax.fori_loop(0, m - 1, foreign_here, 0)
-        for r in range(1, planes):
-            part_out[side, r] = bag_sums(side, r).astype(BF16)
-            part_copy(side, r, planes - r).start()
+        if side == 0:
+            lax.fori_loop(0, m - 1, serve_near, 0)
+        for bag in (1, 0):
+            for r in range(1, planes):
+                part_out[side, r, bag] = bag_sums(side, r, bag).astype(BF16)
+                part_copy(side, r, bag, planes - r).start()
 
     choose(0)
 
@@ -266,14 +272,16 @@
         return 0
 
     lax.fori_loop(0, m - 1, near_here, 0)
-    for side in range(2):
-        total = bag_sums(side, 0)
-        for r in range(1, planes):
-            part_copy(side, r, r).wait()
-            total = total + part_in[side, r].astype(F32)
-        columns = slice(side * half_width, (side + 1) * half_width)
-        query_ref[:, columns] = total[:pairs].astype(BF16)
-        item_ref[:, columns] = total[pairs:]
+
+    def finish(bag, target):
+        for side in range(2):
+            total = bag_sums(side, 0, bag)
+            for r in range(1, planes):
+                part_copy(side, r, bag, r).wait()
+                total = total + part_in[side, r, bag].astype(F32)
+            target[:, side * half_width : (side + 1) * half_width] = total.astype(target.dtype)
+
+    return finish
 
 
 def lookup_scratch(grid, bags, pairs, table):
@@ -288,32 +296,33 @@
         pltpu.VMEM(table.shape, F32),
         pltpu.VMEM((planes, bags, pairs), jnp.int32),
         pltpu.VMEM((128, pairs), F32),
-        pltpu.VMEM((planes, pairs, 128), jnp.int32),
-        pltpu.VMEM((m, planes, 2 * cap), jnp.int32),
-        pltpu.VMEM((m, planes, 2 * cap), jnp.int32),
-        pltpu.SMEM((m, planes, 2 * cap), jnp.int32),
+        pltpu.VMEM((pairs, 128), jnp.int32),
+        pltpu.VMEM((m * planes, 2 * cap), jnp.int32),
+        pltpu.VMEM((m * planes, 1, 2 * cap), jnp.int32),
+        pltpu.VMEM((m * planes, 1, 2 * cap), jnp.int32),
+        pltpu.SMEM((m * planes, 1, 2 * cap), jnp.int32),
         pltpu.VMEM((2, m, planes, cap, width // 2), BF16),
         pltpu.VMEM((2, planes, m, cap, width // 2), BF16),
         pltpu.VMEM((planes, m * cap // chunk, 2 * pairs, chunk), BF16),
         pltpu.VMEM((16, width), F32),
-        pltpu.VMEM((2, planes, 2 * pairs, width // 2), BF16),
-        pltpu.VMEM((2, planes, 2 * pairs, width // 2), BF16),
+        pltpu.VMEM((2, planes, 2, pairs, width // 2), BF16),
+        pltpu.VMEM((2, planes, 2, pairs, width // 2), BF16),
         dma((2,)),
         dma((planes,)),
         dma((planes,)),
-        dma((m,)),
-        dma((m,)),
+        dma((m * planes,)),
+        dma((m * planes,)),
         dma((3, m)),
         dma((3, m)),
-        dma((2, planes)),
-        dma((2, planes)),
+        dma((2, planes, 2)),
+        dma((2, planes, 2)),
     ]
 
 
 def kernel(
     grid, nx, nz, owner_ref, row_ref, table_hbm, first_hbm, second_hbm, loss_ref, item_grad_ref, query_grad_ref,
     query_ref, item_ref, first, second, slope, items, queries, exps, total_out, total_in,
-    query_out, query_in, item_sum, item_out, item_in, acc,
+    query_out, query_in, probs, item_sum, item_out, item_in, acc,
     local_sem, send_sem, recv_sem, *lookup_refs,
 ):
     blk = lax.axis_index("blk")
@@ -342,7 +351,8 @@
                 )
         return nx + nz - 2
 
-    lookup(grid, meet, owner_ref, row_ref, table_hbm, query_ref, item_ref, lookup_refs)
+    finish = lookup(grid, meet, owner_ref, row_ref, table_hbm, lookup_refs)
+    finish(1, item_ref)
     item_unit, item_scale = unit_rows(item_ref[...])
     items[z] = item_unit.astype(BF16)
 
@@ -374,6 +384,7 @@
     for step in range(1, nz):
         item_copy(step, z).start()
 
+    finish(0, query_ref)
     acc[...] = jnp.zeros_like(acc)
     load_first.wait()
     load_second.wait()
@@ -419,29 +430,33 @@
     for step in range(1, nx):
         total_copy(step, along_x(step)[0]).wait_recv()
 
-    all_items = items[...].reshape(nz * pairs, width)
-    query_sum = None
-    for turn in range(nx):
-        step = (turn + 1) % nx
+    for step in range(nx):
         xi = along_x(step)[0]
         total = jnp.zeros((1, pairs), F32)
         for source in range(nx):
             total = total + total_in[source, xi]
         if step == 0:
             loss_ref[...] = jnp.log(total) - own
-        prob = (exps[step].reshape(nz * pairs, pairs) * (1.0 / total)).astype(BF16)
-        part = col_dot(prob, all_items)
-        if step == 0:
-            query_sum = part
-        else:
-            query_out[xi] = part.astype(BF16)
-            query_sum_copy(step, x).start()
-        added = dot(prob, queries[xi]).reshape(nz, pairs, width)
-        item_sum[...] = added if turn == 0 else item_sum[...] + added
+        probs[step] = (exps[step] * (1.0 / total)).astype(BF16)
+
+    def item_part(zi):
+        part = dot(probs[0, zi], queries[x])
+        for step in range(1, nx):
+            part = part + dot(probs[step, zi], queries[along_x(step)[0]])
+        return part
+
+    def query_part(step):
+        return col_dot(probs[step].reshape(nz * pairs, pairs), items[...].reshape(nz * pairs, width))
+
     for step in range(1, nz):
         zi = along_z(step)[0]
-        item_out[zi] = item_sum[zi].astype(BF16)
+        item_out[zi] = item_part(zi).astype(BF16)
         item_sum_copy(step, z).start()
+    for step in range(1, nx):
+        query_out[along_x(step)[0]] = query_part(step).astype(BF16)
+        query_sum_copy(step, x).start()
+    query_sum = query_part(0)
+    item_sum[...] = item_part(z)
 
     for step in range(1, nx):
         xi = along_x(step)[0]
@@ -461,7 +476,7 @@
     lax.fori_loop(0, steps, backward, 0)
     query_grad_ref[...] = acc[...]
 
-    total_items = item_sum[z]
+    total_items = item_sum[...]
     for step in range(1, nz):
         zi = along_z(step)[0]
         item_sum_copy(step, zi).wait_recv()
@@ -508,7 +523,8 @@
             pltpu.VMEM((nx, nx, 1, pairs), F32),
             pltpu.VMEM((nx, pairs, width), BF16),
             pltpu.VMEM((nx, pairs, width), BF16),
-            pltpu.VMEM((nz, pairs, width), F32),
+            pltpu.VMEM((nx, nz, pairs, pairs), BF16),
+            pltpu.VMEM((pairs, width), F32),
             pltpu.VMEM((nz, pairs, width), BF16),
             pltpu.VMEM((nz, pairs, width), BF16),
             pltpu.VMEM((pairs, width), F32),
@@ -518,7 +534,7 @@
             *lookup_scratch(grid, bags, pairs, id_table),
         ],
         compiler_params=pltpu.CompilerParams(
-            collective_id=0, has_side_effects=True, vmem_limit_bytes=60 * 2**20
+            collective_id=0, has_side_effects=True, vmem_limit_bytes=52 * 2**20
         ),
         name="step",
     )(owner_ids.T, row_ids.T, id_table, w_first, w_second)

time: 112 us -> 109 us (0.973)
  the two profiles are of different devices: /device:TPU:8 before, /device:TPU:120 now
where the time goes in v3:
time: 109 us
  Pallas kernels  105 us (96%)
  local copies, waits for them, and re-layouts  3.36 us (3%)
    pallas_call x1, Pallas kernels, local(): pl.pallas_call(functools.partial(kernel, grid, nx, nz), out_shape=(jax.Sh...  105 us
    unnamed x7, local copies, waits for them, and re-layouts  3.36 us

profile of v3, /device:TPU:120, one launch (start us, length us, event | category | flops | bytes accessed | tf_op | source)
XLA Modules:
  0.0 109.0 jit_solution(2055221885807177572)
XLA Ops:
  0.6 0.0 copy-start
  0.6 0.7 copy-done
  1.3 0.0 copy-start.1
  1.3 0.7 copy-done.1
  2.0 105.0 %step.1 = (f32[1,256]{1,0:T(1,128)S(1)}, f32[256,256]{1,0:T(8,128)S(1)}, f32[256,256]{1,0:T(8,128)S(1)}) custom-call(s32[8,256]{1,0:T(8,128)S(1)} %bitcast.3, s32[8,256]{1,0:T(8,128)S(1)} %bitcast.4, bf16[8192,256]{1,0:T(8,128)(2,1)} %table_hbm.1, bf16[256,4096]{1,0:T(8,128)(2,1)} %first_hbm.1, bf16[4096,256]{1,0:T(8,128)(2,1)} %second_hbm.1), custom_call_target="tpu_custom_call" | custom-call | tf_op jit(solution)/shard_map/step/pallas_call | solution.py:504
  107.0 0.6 copy.11
  107.6 0.7 copy.12
  108.3 0.7 copy.13
Async XLA Ops:
  0.6 0.7 copy-start
  1.3 0.7 copy-start.1

commit v4 on v3

--- a/solution.py
+++ b/solution.py
@@ -36,12 +36,12 @@
     return scale * (grad - unit * jnp.sum(unit * grad, axis=-1, keepdims=True))
 
 
-def lookup(grid, meet, owner_ref, row_ref, table_ref, refs):
+def lookup(grid, meet, packed_ref, table_ref, refs):
     ny, planes, cores = grid
     (table_bf, table_wide, ids, code_rows, codes, req_all, req_out, req_in, req_smem, rows_out, rows_in, select,
      stage, part_out, part_in, local_sem, ids_send, ids_recv, req_send, req_recv, rows_send, rows_recv,
-     part_send, part_recv) = refs
-    bags, pairs = owner_ref.shape
+     part_send, part_recv, smem_sem) = refs
+    bags, pairs = packed_ref.shape
     shard_rows, width = table_ref.shape
     cap, half_width = rows_in.shape[3:]
     chunks, chunk = select.shape[1], select.shape[3]
@@ -66,15 +66,16 @@
         away = m // 2 - (step + 1) // 2
         return lax.rem(q + away + (step % 2) * (m - 2 * away), m)
 
-    def further(step):
-        return lax.rem(t + step, n)
+    def asker(place, r):
+        return shard(place, lax.rem(plane + r, planes))
 
     fetch = pltpu.make_async_copy(table_ref, table_bf, local_sem.at[0])
     fetch.start()
     barrier = pltpu.get_barrier_semaphore()
 
     def greet(step, _):
-        pl.semaphore_signal(barrier, inc=1, device_id={"table": further(step)}, device_id_type=MESH)
+        other = lax.rem(t + step, n)
+        pl.semaphore_signal(barrier, inc=1, device_id={"table": other}, device_id_type=MESH)
         return 0
 
     lax.fori_loop(1, n, greet, 0)
@@ -91,17 +92,18 @@
         < lax.broadcasted_iota(jnp.int32, (pairs, pairs), 1),
         1.0, 0.0,
     ).astype(BF16)
+    bits = shard_rows.bit_length() - 1
     count = jnp.zeros((n, 1), F32)
     wanted = jnp.zeros((n, 2 * cap), F32)
     for k in range(bags):
-        hot = jnp.where(owner_ref[k : k + 1, :] == shard_iota, 1.0, 0.0)
+        packed = packed_ref[k : k + 1, :]
+        hot = jnp.where(packed >> bits == shard_iota, 1.0, 0.0)
         hot_bf = hot.astype(BF16)
         held = dot(hot_bf, earlier) + count
         slot = jnp.sum(hot * held, axis=0, keepdims=True)
         code = slot + jnp.sum(hot * first_slot, axis=0, keepdims=True)
         ids[0, k : k + 1, :] = code.astype(jnp.int32)
-        row = row_ref[k : k + 1, :]
-        digit = jnp.where(low_digit, row & 127, row >> 7).astype(F32)
+        digit = jnp.where(low_digit, packed & 127, (packed & (shard_rows - 1)) >> 7).astype(F32)
         digit = jnp.where(digit_slot == slot, digit, 0.0).astype(BF16)
         wanted = wanted + row_dot(hot_bf, digit)
         count = count + jnp.sum(hot, axis=1, keepdims=True)
@@ -112,21 +114,25 @@
         return 0
 
     lax.fori_loop(0, n, split, 0)
-    req_in[t] = req_out[t]
     pl.semaphore_wait(barrier, n - 1 + others)
 
-    def request(to, slot):
+    def request(place, r, slot, slot_r):
+        to = asker(place, r)
         return pltpu.make_async_remote_copy(
-            src_ref=req_out.at[to], dst_ref=req_in.at[slot],
-            send_sem=req_send.at[to], recv_sem=req_recv.at[slot],
+            src_ref=req_out.at[to], dst_ref=req_in.at[slot, slot_r],
+            send_sem=req_send.at[place, r], recv_sem=req_recv.at[slot, slot_r],
             device_id={"table": to}, device_id_type=MESH,
         )
 
     def ask(step, _):
-        request(further(step), t).start()
-        return 0
-
-    lax.fori_loop(1, n, ask, 0)
+        for r in (*range(1, planes), 0):
+            request(around(step), r, q, (planes - r) % planes).start()
+        return 0
+
+    lax.fori_loop(0, m - 1, ask, 0)
+    for r in range(1, planes):
+        request(q, r, q, planes - r).start()
+    req_in[q, 0] = req_out[t]
 
     def ids_copy(r, slot):
         return pltpu.make_async_remote_copy(
@@ -148,21 +154,18 @@
 
     lax.fori_loop(0, blocks, widen, 0)
 
-    def asked(step, _):
-        request(further(step), further(step)).wait()
-        return 0
-
-    lax.fori_loop(1, n, asked, 0)
-    to_smem = pltpu.make_async_copy(req_in, req_smem, local_sem.at[1])
-    to_smem.start()
-    to_smem.wait()
+    def to_smem(place):
+        return pltpu.make_async_copy(req_in.at[place], req_smem.at[place], smem_sem.at[place])
+
+    def asked(place):
+        for r in range(planes):
+            request(place, r, place, r).wait()
+        to_smem(place).start()
 
     def gather(place, r, left, right):
-        asker = shard(place, lax.rem(plane + r, planes))
-
         def some(part, _):
             for s in range(step_rows):
-                index = req_smem[asker, 0, part * step_rows + s] & (shard_rows - 1)
+                index = req_smem[place, r, 0, part * step_rows + s] & (shard_rows - 1)
                 stage[s : s + 1, :] = table_wide[pl.ds(index, 1), :]
             at = pl.ds(pl.multiple_of(part * step_rows, step_rows), step_rows)
             rows = stage[...].astype(BF16)
@@ -190,6 +193,12 @@
 
     def serve_foreign(step, _):
         place = around(step)
+
+        @pl.when(step < m - 2)
+        def _():
+            asked(around(step + 1))
+
+        to_smem(place).wait()
         for r in range(1, planes):
             gather(place, r, rows_out.at[0, place, r], rows_out.at[1, place, r])
         foreign_copy(0, place, q).start()
@@ -208,8 +217,13 @@
         near_copy(around(step), q).start()
         return 0
 
+    asked(around(0))
     lax.fori_loop(0, m - 1, serve_foreign, 0)
     lax.fori_loop(0, m - 1, serve_second, 0)
+    for r in range(1, planes):
+        request(q, r, q, r).wait()
+    to_smem(q).start()
+    to_smem(q).wait()
     for r in range(planes):
         gather(q, r, rows_in.at[0, r, q], rows_in.at[1, r, q])
     lax.fori_loop(0, m - 1, collect_near, 0)
@@ -256,9 +270,12 @@
             foreign_copy(side, place, place).wait()
             return 0
 
-        lax.fori_loop(0, m - 1, foreign_here, 0)
-        if side == 0:
+        if side == 1:
+            lax.fori_loop(0, 2 * m // 3, foreign_here, 0)
             lax.fori_loop(0, m - 1, serve_near, 0)
+            lax.fori_loop(2 * m // 3, m - 1, foreign_here, 0)
+        else:
+            lax.fori_loop(0, m - 1, foreign_here, 0)
         for bag in (1, 0):
             for r in range(1, planes):
                 part_out[side, r, bag] = bag_sums(side, r, bag).astype(BF16)
@@ -299,8 +316,8 @@
         pltpu.VMEM((pairs, 128), jnp.int32),
         pltpu.VMEM((m * planes, 2 * cap), jnp.int32),
         pltpu.VMEM((m * planes, 1, 2 * cap), jnp.int32),
-        pltpu.VMEM((m * planes, 1, 2 * cap), jnp.int32),
-        pltpu.SMEM((m * planes, 1, 2 * cap), jnp.int32),
+        pltpu.VMEM((m, planes, 1, 2 * cap), jnp.int32),
+        pltpu.SMEM((m, planes, 1, 2 * cap), jnp.int32),
         pltpu.VMEM((2, m, planes, cap, width // 2), BF16),
         pltpu.VMEM((2, planes, m, cap, width // 2), BF16),
         pltpu.VMEM((planes, m * cap // chunk, 2 * pairs, chunk), BF16),
@@ -310,17 +327,18 @@
         dma((2,)),
         dma((planes,)),
         dma((planes,)),
-        dma((m * planes,)),
-        dma((m * planes,)),
+        dma((m, planes)),
+        dma((m, planes)),
         dma((3, m)),
         dma((3, m)),
         dma((2, planes, 2)),
         dma((2, planes, 2)),
+        dma((m,)),
     ]
 
 
 def kernel(
-    grid, nx, nz, owner_ref, row_ref, table_hbm, first_hbm, second_hbm, loss_ref, item_grad_ref, query_grad_ref,
+    grid, nx, nz, packed_ref, table_hbm, first_hbm, second_hbm, loss_ref, item_grad_ref, query_grad_ref,
     query_ref, item_ref, first, second, slope, items, queries, exps, total_out, total_in,
     query_out, query_in, probs, item_sum, item_out, item_in, acc,
     local_sem, send_sem, recv_sem, *lookup_refs,
@@ -351,7 +369,7 @@
                 )
         return nx + nz - 2
 
-    finish = lookup(grid, meet, owner_ref, row_ref, table_hbm, lookup_refs)
+    finish = lookup(grid, meet, packed_ref, table_hbm, lookup_refs)
     finish(1, item_ref)
     item_unit, item_scale = unit_rows(item_ref[...])
     items[z] = item_unit.astype(BF16)
@@ -508,7 +526,7 @@
             jax.ShapeDtypeStruct((pairs, width), F32),
             jax.ShapeDtypeStruct((pairs, width), F32),
         ),
-        in_specs=[vmem, vmem, hbm, hbm, hbm],
+        in_specs=[vmem, hbm, hbm, hbm],
         out_specs=(vmem, vmem, vmem),
         scratch_shapes=[
             pltpu.VMEM((pairs, width), BF16),
@@ -537,7 +555,7 @@
             collective_id=0, has_side_effects=True, vmem_limit_bytes=52 * 2**20
         ),
         name="step",
-    )(owner_ids.T, row_ids.T, id_table, w_first, w_second)
+    )((owner_ids * id_table.shape[0] + row_ids).T, id_table, w_first, w_second)
     return loss.reshape(-1), item_grad, query_grad
 
 

time: 109 us -> 107 us (0.982)
  the two profiles are of different devices: /device:TPU:120 before, /device:TPU:24 now
where the time goes in v4:
time: 107 us
  Pallas kernels  104 us (97%)
  local copies, waits for them, and re-layouts  1.97 us (2%)
    pallas_call x1, Pallas kernels, local(): pl.pallas_call(functools.partial(kernel, grid, nx, nz), out_shape=(jax.Sh...  104 us

profile of v4, /device:TPU:24, one launch (start us, length us, event | category | flops | bytes accessed | tf_op | source)
XLA Modules:
  0.0 106.9 jit_solution(1627369105521625714)
XLA Ops:
  0.6 0.7 add_bitcast_fusion.packed_ref
  1.3 103.6 %step.1 = (f32[1,256]{1,0:T(1,128)S(1)}, f32[256,256]{1,0:T(8,128)S(1)}, f32[256,256]{1,0:T(8,128)S(1)}) custom-call(s32[8,256]{1,0:T(8,128)S(1)} %add_bitcast_fusion.packed_ref, bf16[8192,256]{1,0:T(8,128)(2,1)} %table_hbm.1, bf16[256,4096]{1,0:T(8,128)(2,1)} %first_hbm.1, bf16[4096,256]{1,0:T(8,128)(2,1)} %second_hbm.1), custom_call_target="tpu_custom_call" | custom-call | tf_op jit(solution)/shard_map/step/pallas_call | solution.py:522
  104.9 0.6 copy.11
  105.5 0.7 copy.12
  106.2 0.7 copy.13

commit v5 on v4

--- a/solution.py
+++ b/solution.py
@@ -36,7 +36,7 @@
     return scale * (grad - unit * jnp.sum(unit * grad, axis=-1, keepdims=True))
 
 
-def lookup(grid, meet, packed_ref, table_ref, refs):
+def lookup(grid, meet, load, packed_ref, table_ref, refs):
     ny, planes, cores = grid
     (table_bf, table_wide, ids, code_rows, codes, req_all, req_out, req_in, req_smem, rows_out, rows_in, select,
      stage, part_out, part_in, local_sem, ids_send, ids_recv, req_send, req_recv, rows_send, rows_recv,
@@ -69,8 +69,15 @@
     def asker(place, r):
         return shard(place, lax.rem(plane + r, planes))
 
-    fetch = pltpu.make_async_copy(table_ref, table_bf, local_sem.at[0])
-    fetch.start()
+    pieces = 8
+    piece_rows = shard_rows // pieces
+
+    def fetch(piece):
+        at = pl.ds(piece * piece_rows, piece_rows)
+        return pltpu.make_async_copy(table_ref.at[at, :], table_bf.at[at, :], local_sem.at[piece])
+
+    for piece in range(pieces):
+        fetch(piece).start()
     barrier = pltpu.get_barrier_semaphore()
 
     def greet(step, _):
@@ -143,16 +150,18 @@
     for r in range(1, planes):
         ids_copy(r, planes - r).start()
 
-    fetch.wait()
-    blocks = 32
-    block_rows = shard_rows // blocks
-
-    def widen(block, _):
-        at = pl.ds(pl.multiple_of(block * block_rows, block_rows), block_rows)
-        table_wide[at, :] = table_bf[at, :].astype(F32)
-        return 0
-
-    lax.fori_loop(0, blocks, widen, 0)
+    blocks = 4
+    block_rows = piece_rows // blocks
+    for piece in range(pieces):
+        fetch(piece).wait()
+
+        def widen(block, _):
+            at = pl.ds(pl.multiple_of(piece * piece_rows + block * block_rows, block_rows), block_rows)
+            table_wide[at, :] = table_bf[at, :].astype(F32)
+            return 0
+
+        lax.fori_loop(0, blocks, widen, 0)
+    load()
 
     def to_smem(place):
         return pltpu.make_async_copy(req_in.at[place], req_smem.at[place], smem_sem.at[place])
@@ -226,7 +235,6 @@
     to_smem(q).wait()
     for r in range(planes):
         gather(q, r, rows_in.at[0, r, q], rows_in.at[1, r, q])
-    lax.fori_loop(0, m - 1, collect_near, 0)
 
     code_rows[...] = jnp.zeros_like(code_rows)
 
@@ -271,6 +279,7 @@
             return 0
 
         if side == 1:
+            lax.fori_loop(0, m - 1, collect_near, 0)
             lax.fori_loop(0, 2 * m // 3, foreign_here, 0)
             lax.fori_loop(0, m - 1, serve_near, 0)
             lax.fori_loop(2 * m // 3, m - 1, foreign_here, 0)
@@ -324,7 +333,7 @@
         pltpu.VMEM((16, width), F32),
         pltpu.VMEM((2, planes, 2, pairs, width // 2), BF16),
         pltpu.VMEM((2, planes, 2, pairs, width // 2), BF16),
-        dma((2,)),
+        dma((8,)),
         dma((planes,)),
         dma((planes,)),
         dma((m, planes)),
@@ -350,8 +359,10 @@
 
     load_first = pltpu.make_async_copy(first_hbm, first, local_sem.at[0])
     load_second = pltpu.make_async_copy(second_hbm, second, local_sem.at[1])
-    load_first.start()
-    load_second.start()
+
+    def load():
+        load_first.start()
+        load_second.start()
 
     def along_x(step):
         there = lax.rem(x + step, nx)
@@ -369,7 +380,7 @@
                 )
         return nx + nz - 2
 
-    finish = lookup(grid, meet, packed_ref, table_hbm, lookup_refs)
+    finish = lookup(grid, meet, load, packed_ref, table_hbm, lookup_refs)
     finish(1, item_ref)
     item_unit, item_scale = unit_rows(item_ref[...])
     items[z] = item_unit.astype(BF16)
@@ -425,29 +436,32 @@
         jnp.int32, (pairs, pairs), 1
     )
 
+    part = jnp.zeros((1, pairs), F32)
     own = None
-    for step in range(nx):
+    for turn in range(nz):
+        zi = along_z(turn)[0]
+        if turn > 0:
+            item_copy(turn, zi).wait_recv()
+        scores = INV_TEMP * row_dot(items[zi], queries[x])
+        if turn == 0:
+            own = jnp.sum(jnp.where(diagonal, scores, 0.0), axis=0, keepdims=True)
+        value = jnp.exp(scores)
+        exps[0, zi] = value
+        part = part + jnp.sum(value, axis=0, keepdims=True)
+    total_out[x] = part
+    for step in range(1, nx):
         xi = along_x(step)[0]
-        if step > 0:
-            query_copy(step, xi).wait_recv()
-        part = jnp.zeros((1, pairs), F32)
-        for turn in range(nz):
-            zi = along_z(turn)[0]
-            if step == 0 and turn > 0:
-                item_copy(turn, zi).wait_recv()
-            scores = INV_TEMP * row_dot(items[zi], queries[xi])
-            if step == 0 and turn == 0:
-                own = jnp.sum(jnp.where(diagonal, scores, 0.0), axis=0, keepdims=True)
-            value = jnp.exp(scores)
-            exps[step, zi] = value
-            part = part + jnp.sum(value, axis=0, keepdims=True)
-        total_out[xi] = part
+        query_copy(step, xi).wait_recv()
+        value = jnp.exp(INV_TEMP * row_dot(items[...].reshape(nz * pairs, width), queries[xi]))
+        exps[step] = value.reshape(nz, pairs, pairs)
+        total_out[xi] = jnp.sum(value, axis=0, keepdims=True)
     total_in[x] = total_out[...]
     for step in range(1, nx):
         total_copy(step, x).start()
     for step in range(1, nx):
         total_copy(step, along_x(step)[0]).wait_recv()
 
+    inverse = []
     for step in range(nx):
         xi = along_x(step)[0]
         total = jnp.zeros((1, pairs), F32)
@@ -455,12 +469,14 @@
             total = total + total_in[source, xi]
         if step == 0:
             loss_ref[...] = jnp.log(total) - own
-        probs[step] = (exps[step] * (1.0 / total)).astype(BF16)
+        inverse.append(1.0 / total)
 
     def item_part(zi):
-        part = dot(probs[0, zi], queries[x])
-        for step in range(1, nx):
-            part = part + dot(probs[step, zi], queries[along_x(step)[0]])
+        part = jnp.zeros((pairs, width), F32)
+        for step in range(nx):
+            prob = (exps[step, zi] * inverse[step]).astype(BF16)
+            probs[step, zi] = prob
+            part = part + dot(prob, queries[along_x(step)[0]])
         return part
 
     def query_part(step):
@@ -470,11 +486,11 @@
         zi = along_z(step)[0]
         item_out[zi] = item_part(zi).astype(BF16)
         item_sum_copy(step, z).start()
+    item_sum[...] = item_part(z)
     for step in range(1, nx):
         query_out[along_x(step)[0]] = query_part(step).astype(BF16)
         query_sum_copy(step, x).start()
     query_sum = query_part(0)
-    item_sum[...] = item_part(z)
 
     for step in range(1, nx):
         xi = along_x(step)[0]

time: 107 us -> 105 us (0.981)
  the two profiles are of different devices: /device:TPU:24 before, /device:TPU:2 now
where the time goes in v5:
time: 105 us
  Pallas kernels  102 us (97%)
  local copies, waits for them, and re-layouts  1.97 us (2%)
    pallas_call x1, Pallas kernels, local(): pl.pallas_call(functools.partial(kernel, grid, nx, nz), out_shape=(jax.Sh...  102 us

profile of v5, /device:TPU:2, one launch (start us, length us, event | category | flops | bytes accessed | tf_op | source)
XLA Modules:
  0.0 104.9 jit_solution(7181656923079533051)
XLA Ops:
  0.6 0.7 add_bitcast_fusion.packed_ref
  1.3 101.6 %step.1 = (f32[1,256]{1,0:T(1,128)S(1)}, f32[256,256]{1,0:T(8,128)S(1)}, f32[256,256]{1,0:T(8,128)S(1)}) custom-call(s32[8,256]{1,0:T(8,128)S(1)} %add_bitcast_fusion.packed_ref, bf16[8192,256]{1,0:T(8,128)(2,1)} %table_hbm.1, bf16[256,4096]{1,0:T(8,128)(2,1)} %first_hbm.1, bf16[4096,256]{1,0:T(8,128)(2,1)} %second_hbm.1), custom_call_target="tpu_custom_call" | custom-call | tf_op jit(solution)/shard_map/step/pallas_call | solution.py:538
  102.9 0.6 copy.11
  103.5 0.7 copy.12
  104.2 0.7 copy.13

commit v6 on v5

--- a/solution.py
+++ b/solution.py
@@ -349,7 +349,7 @@
 def kernel(
     grid, nx, nz, packed_ref, table_hbm, first_hbm, second_hbm, loss_ref, item_grad_ref, query_grad_ref,
     query_ref, item_ref, first, second, slope, items, queries, exps, total_out, total_in,
-    query_out, query_in, probs, item_sum, item_out, item_in, acc,
+    query_out, query_in, probs, item_sum, item_out, item_in, passed, acc,
     local_sem, send_sem, recv_sem, *lookup_refs,
 ):
     blk = lax.axis_index("blk")
@@ -410,8 +410,32 @@
         there = along_z(step)[0]
         return copy(4, item_out.at[there], item_in.at[slot], slot, step, along_z)
 
-    for step in range(1, nz):
-        item_copy(step, z).start()
+    middle = (z == 1) | (z == 2)
+    end = (z == 0) | (z == 3)
+    far = 3 * (2 - z)
+
+    def not_across(step):
+        return middle | (z + along_z(step)[0] != 3)
+
+    def item_forward():
+        return pltpu.make_async_remote_copy(
+            src_ref=items.at[far], dst_ref=items.at[far],
+            send_sem=send_sem.at[0, z], recv_sem=recv_sem.at[0, far],
+            device_id={"blk": x * nz + 3 - far}, device_id_type=MESH,
+        )
+
+    def item_pass():
+        between = 1 + z // 3
+        return pltpu.make_async_remote_copy(
+            src_ref=item_out.at[3 - z], dst_ref=passed,
+            send_sem=send_sem.at[5, 0], recv_sem=recv_sem.at[5, 0],
+            device_id={"blk": x * nz + between}, device_id_type=MESH,
+        )
+
+    for step in (2, 1, 3):
+        @pl.when(not_across(step))
+        def _():
+            item_copy(step, z).start()
 
     finish(0, query_ref)
     acc[...] = jnp.zeros_like(acc)
@@ -432,6 +456,11 @@
     for step in range(1, nx):
         query_copy(step, x).start()
 
+    @pl.when(middle)
+    def _():
+        item_copy(2, far).wait_recv()
+        item_forward().start()
+
     diagonal = lax.broadcasted_iota(jnp.int32, (pairs, pairs), 0) == lax.broadcasted_iota(
         jnp.int32, (pairs, pairs), 1
     )
@@ -440,7 +469,11 @@
     own = None
     for turn in range(nz):
         zi = along_z(turn)[0]
-        if turn > 0:
+        if turn == 2:
+            @pl.when(end)
+            def _():
+                item_copy(turn, zi).wait_recv()
+        elif turn > 0:
             item_copy(turn, zi).wait_recv()
         scores = INV_TEMP * row_dot(items[zi], queries[x])
         if turn == 0:
@@ -482,15 +515,47 @@
     def query_part(step):
         return col_dot(probs[step].reshape(nz * pairs, pairs), items[...].reshape(nz * pairs, width))
 
-    for step in range(1, nz):
-        zi = along_z(step)[0]
-        item_out[zi] = item_part(zi).astype(BF16)
-        item_sum_copy(step, z).start()
-    item_sum[...] = item_part(z)
+    def item_sum_to(there):
+        return pltpu.make_async_remote_copy(
+            src_ref=item_out.at[there], dst_ref=item_in.at[z],
+            send_sem=send_sem.at[4, there], recv_sem=recv_sem.at[4, z],
+            device_id={"blk": x * nz + there}, device_id_type=MESH,
+        )
+
+    first_to, second_to = 3 - z, (2 + 3 * z) % 5
+    third_to = 6 - z - first_to - second_to
+    item_out[first_to] = item_part(first_to).astype(BF16)
+
+    @pl.when(middle)
+    def _():
+        item_sum_to(first_to).start()
+
+    @pl.when(end)
+    def _():
+        item_pass().start()
+
+    item_out[second_to] = item_part(second_to).astype(BF16)
+    item_sum_to(second_to).start()
+    item_sum[...] = item_part(third_to)
+
+    @pl.when(end)
+    def _():
+        item_out[third_to] = item_sum[...].astype(BF16)
+        item_sum_to(third_to).start()
+
+    own_part = item_part(z)
     for step in range(1, nx):
         query_out[along_x(step)[0]] = query_part(step).astype(BF16)
         query_sum_copy(step, x).start()
     query_sum = query_part(0)
+
+    @pl.when(middle)
+    def _():
+        item_pass().wait_recv()
+        item_out[third_to] = (item_sum[...] + passed[...].astype(F32)).astype(BF16)
+        item_sum_to(third_to).start()
+
+    item_sum[...] = own_part
 
     for step in range(1, nx):
         xi = along_x(step)[0]
@@ -510,18 +575,31 @@
     lax.fori_loop(0, steps, backward, 0)
     query_grad_ref[...] = acc[...]
 
+    for step in range(1, nz):
+        @pl.when(not_across(step))
+        def _():
+            zi = along_z(step)[0]
+            item_sum_copy(step, zi).wait_recv()
+            item_sum[...] += item_in[zi].astype(F32)
     total_items = item_sum[...]
-    for step in range(1, nz):
-        zi = along_z(step)[0]
-        item_sum_copy(step, zi).wait_recv()
-        total_items = total_items + item_in[zi].astype(F32)
     item_unit_grad = INV_TEMP * (total_items - queries[x].astype(F32))
     item_unit, item_scale = unit_rows(item_ref[...])
     item_grad_ref[...] = unit_backward(item_unit_grad, item_unit, item_scale)
 
     for step in range(1, nz):
-        item_copy(step, z).wait_send()
-        item_sum_copy(step, z).wait_send()
+        @pl.when(not_across(step))
+        def _():
+            item_copy(step, z).wait_send()
+            item_sum_copy(step, z).wait_send()
+
+    @pl.when(middle)
+    def _():
+        item_forward().wait_send()
+
+    @pl.when(end)
+    def _():
+        item_pass().wait_send()
+
     for step in range(1, nx):
         query_copy(step, x).wait_send()
         total_copy(step, x).wait_send()
@@ -561,10 +639,11 @@
             pltpu.VMEM((pairs, width), F32),
             pltpu.VMEM((nz, pairs, width), BF16),
             pltpu.VMEM((nz, pairs, width), BF16),
+            pltpu.VMEM((pairs, width), BF16),
             pltpu.VMEM((pairs, width), F32),
             pltpu.SemaphoreType.DMA((2,)),
-            pltpu.SemaphoreType.DMA((5, most)),
-            pltpu.SemaphoreType.DMA((5, most)),
+            pltpu.SemaphoreType.DMA((6, most)),
+            pltpu.SemaphoreType.DMA((6, most)),
             *lookup_scratch(grid, bags, pairs, id_table),
         ],
         compiler_params=pltpu.CompilerParams(

time: 105 us -> 105 us (level)
  no operation moved by 1% of the time
where the time goes in v6:
time: 105 us
  Pallas kernels  102 us (97%)
  local copies, waits for them, and re-layouts  1.97 us (2%)
    pallas_call x1, Pallas kernels, local(): pl.pallas_call(functools.partial(kernel, grid, nx, nz), out_shape=(jax.Sh...  102 us

profile of v6, /device:TPU:2, one launch (start us, length us, event | category | flops | bytes accessed | tf_op | source)
XLA Modules:
  0.0 105.1 jit_solution(2309255529379491013)
XLA Ops:
  0.6 0.7 add_bitcast_fusion.packed_ref
  1.3 101.7 %step.1 = (f32[1,256]{1,0:T(1,128)S(1)}, f32[256,256]{1,0:T(8,128)S(1)}, f32[256,256]{1,0:T(8,128)S(1)}) custom-call(s32[8,256]{1,0:T(8,128)S(1)} %add_bitcast_fusion.packed_ref, bf16[8192,256]{1,0:T(8,128)(2,1)} %table_hbm.1, bf16[256,4096]{1,0:T(8,128)(2,1)} %first_hbm.1, bf16[4096,256]{1,0:T(8,128)(2,1)} %second_hbm.1), custom_call_target="tpu_custom_call" | custom-call | tf_op jit(solution)/shard_map/step/pallas_call | solution.py:616
  103.1 0.6 copy.11
  103.6 0.7 copy.12
  104.3 0.7 copy.13

commit v7 on v5

--- a/solution.py
+++ b/solution.py
@@ -330,7 +330,7 @@
         pltpu.VMEM((2, m, planes, cap, width // 2), BF16),
         pltpu.VMEM((2, planes, m, cap, width // 2), BF16),
         pltpu.VMEM((planes, m * cap // chunk, 2 * pairs, chunk), BF16),
-        pltpu.VMEM((16, width), F32),
+        pltpu.VMEM((32, width), F32),
         pltpu.VMEM((2, planes, 2, pairs, width // 2), BF16),
         pltpu.VMEM((2, planes, 2, pairs, width // 2), BF16),
         dma((8,)),
@@ -531,7 +531,7 @@
 def local(grid, nx, nz, id_table, w_first, w_second, owner_ids, row_ids):
     pairs, bags = owner_ids.shape
     width, hidden = w_first.shape
-    chunk = min(hidden, 512)
+    chunk = min(hidden, 1024)
     vmem = pl.BlockSpec(memory_space=pltpu.VMEM)
     hbm = pl.BlockSpec(memory_space=pltpu.HBM)
     most = max(nx, nz)

time: 105 us -> 104 us (level)
  the two profiles are of different devices: /device:TPU:2 before, /device:TPU:64 now
where the time goes in v7:
time: 104 us
  Pallas kernels  100 us (96%)
  local copies, waits for them, and re-layouts  1.97 us (2%)
    pallas_call x1, Pallas kernels, local(): pl.pallas_call(functools.partial(kernel, grid, nx, nz), out_shape=(jax.Sh...  100 us

profile of v7, /device:TPU:64, one launch (start us, length us, event | category | flops | bytes accessed | tf_op | source)
XLA Modules:
  0.0 103.6 jit_solution(14168286094553365819)
XLA Ops:
  0.6 0.7 add_bitcast_fusion.packed_ref
  1.3 100.3 %step.1 = (f32[1,256]{1,0:T(1,128)S(1)}, f32[256,256]{1,0:T(8,128)S(1)}, f32[256,256]{1,0:T(8,128)S(1)}) custom-call(s32[8,256]{1,0:T(8,128)S(1)} %add_bitcast_fusion.packed_ref, bf16[8192,256]{1,0:T(8,128)(2,1)} %table_hbm.1, bf16[256,4096]{1,0:T(8,128)(2,1)} %first_hbm.1, bf16[4096,256]{1,0:T(8,128)(2,1)} %second_hbm.1), custom_call_target="tpu_custom_call" | custom-call | tf_op jit(solution)/shard_map/step/pallas_call | solution.py:538
  101.6 0.6 copy.11
  102.2 0.7 copy.12
  102.9 0.7 copy.13
